TPU v7x, 256 devices: a whole 4x4x8 slice. The times are simulated.
256 devices in a mesh: dp: 16 (over z, core), group: 16 (over x, y).
Axes of the slice: x: 4, y: 4, z: 8, core: 2. Of those that a mesh axis runs over, the one named last changes fastest.
Arguments:
- features: bfloat16 [524288, 512], P(('dp', 'group')), parts along dimension 0, may hold values from -36.2 to 36.2
- proj_weight: bfloat16 [512, 256], replicated, may hold values from -0.25 to 0.25
- class_weight: bfloat16 [8192, 124], P('dp'), parts along dimension 0, may hold values from -0.1777767 to 0.1777767
- anchor_blocks: int32 [256], P('dp'), parts along dimension 0, may hold values from 1 to 4, as said below
- anchor_pix: int32 [256, 512], P(('dp', 'group')), parts along dimension 0, may hold values from 0 to 2047, as said below
- anchor_label: int32 [256, 512], P('dp'), parts along dimension 0, may hold values from 0 to 123
- pixel_label: int32 [524288], P(('dp', 'group')), parts along dimension 0, may hold values from 0 to 123
Outputs:
- grad_features: bfloat16 [524288, 512], P(('dp', 'group')), parts along dimension 0
- grad_proj: float32 [8192, 256], P('dp'), parts along dimension 0
- grad_class: float32 [8192, 124], P('dp'), parts along dimension 0
- losses: float32 [32], P('dp'), parts along dimension 0
There are 16 independent parts, one for each index of `dp`. A program takes and returns all parts, laid end to end along the dimension named above; an argument that names none is the same for every part. Nothing has to cross between parts.
Inputs may be any that keep to these rules, and one draw needn't show every extreme that they name: Anchor rows of image g at slots 128 * anchor_blocks[g] and beyond are unused. `anchor_pix`: within one image the pixel indices of the slots are distinct.
All inputs are finite; a program needn't handle non-finite values.
Results may differ from a plain program's by a relative error of at most 0.0037.
Values may be sent and summed in bfloat16 or wider, within the bound.
No kernel may reach another device: no remote copies, remote signals or barrier semaphores. Data moves between devices by JAX's collectives and lax.ppermute only.
A program may use at most 128 MiB of HBM per device.

v0:
```python
import jax
import jax.numpy as jnp
from jax import lax
from jax.sharding import PartitionSpec as P

BLK = 128


INV_TEMP = 10.0
CONTRAST_WEIGHT = 0.1
NORM_EPS = 1e-06


def pair_scores(left, right):
    return lax.dot_general(
        left, right, (((1,), (1,)), ((), ())), preferred_element_type=jnp.float32
    )


def column_sum(left, right):
    return lax.dot_general(
        left, right, (((0,), (0,)), ((), ())), preferred_element_type=jnp.float32
    )


def exact_pair(left, right):
    return lax.dot_general(
        left,
        right,
        (((1,), (1,)), ((), ())),
        precision=lax.Precision.HIGHEST,
        preferred_element_type=jnp.float32,
    )


def exact_column(left, right):
    return lax.dot_general(
        left,
        right,
        (((0,), (0,)), ((), ())),
        precision=lax.Precision.HIGHEST,
        preferred_element_type=jnp.float32,
    )


def row_terms(queries, row_ids, query_labels, query_keep, key_rows, key_labels, key_keep):
    scores = pair_scores(queries, key_rows) * INV_TEMP
    column_ids = jnp.arange(key_rows.shape[0], dtype=jnp.int32)
    allowed = key_keep[None, :] & (column_ids[None, :] != row_ids[:, None])
    totals = jnp.sum(jnp.where(allowed, jnp.exp(scores - INV_TEMP), 0.0), axis=1)
    logsum = jnp.log(totals) + INV_TEMP
    same_mask = (allowed & (query_labels[:, None] == key_labels[None, :])).astype(jnp.float32)
    pos_count = jnp.sum(same_mask, axis=1)
    pos_floor = jnp.maximum(pos_count, 1.0)
    keep_float = query_keep.astype(jnp.float32)
    anchor_loss = (
        keep_float * (pos_count * logsum - jnp.sum(same_mask * scores, axis=1)) / pos_floor
    )
    return (scores, allowed, same_mask, logsum, pos_count, keep_float, anchor_loss)


def coefficients(scores, allowed, same_mask, logsum, pos_count, keep_float):
    pos_floor = jnp.maximum(pos_count, 1.0)
    pos_ratio = pos_count / pos_floor
    probable = jnp.where(allowed, jnp.exp(scores - logsum), 0.0)
    scaled = (
        CONTRAST_WEIGHT * INV_TEMP * keep_float * (pos_ratio * probable - same_mask / pos_floor)
    )
    return scaled.astype(jnp.bfloat16)


def per_device(
    features, proj_weight, class_weight, anchor_blocks, anchor_pix, anchor_label, pixel_label
):
    groups = lax.axis_size("group")
    my_index = lax.axis_index("group")
    slot_count = anchor_pix.shape[1]
    pixel_count = features.shape[0]
    channels = features.shape[1]
    pix_ids = anchor_pix[0]
    picked = features[pix_ids]
    projected = jnp.dot(picked, proj_weight, preferred_element_type=jnp.float32)
    length = jnp.sqrt(jnp.sum(projected * projected, axis=1, keepdims=True) + NORM_EPS)
    unit_rows = projected / length
    embedded = unit_rows.astype(jnp.bfloat16)
    gathered = lax.all_gather(embedded, "group", axis=0, tiled=True)
    emb_width = gathered.shape[1]
    total_rows = gathered.shape[0]
    row_limit = jnp.broadcast_to((anchor_blocks * BLK)[:, None], (groups, slot_count)).reshape(-1)
    slot_ids = jnp.broadcast_to(
        jnp.arange(slot_count, dtype=jnp.int32)[None, :], (groups, slot_count)
    ).reshape(-1)
    keep_mask = slot_ids < row_limit
    label_rows = anchor_label.reshape(-1)
    group_ids = jnp.arange(groups, dtype=jnp.int32)
    own_blocks = jnp.sum(jnp.where(group_ids == my_index, anchor_blocks, 0))
    own_start = my_index * slot_count
    logits = jnp.dot(features, class_weight, preferred_element_type=jnp.float32)
    top_logit = jnp.max(logits, axis=1, keepdims=True)
    logsum_class = jnp.log(jnp.sum(jnp.exp(logits - top_logit), axis=1, keepdims=True)) + top_logit
    onehot = (pixel_label[:, None] == jnp.arange(logits.shape[1], dtype=jnp.int32)[None, :]).astype(
        jnp.float32
    )
    pixel_loss = logsum_class[:, 0] - jnp.sum(onehot * logits, axis=1)
    grad_logits = (jnp.exp(logits - logsum_class) - onehot).astype(jnp.bfloat16)
    class_part = column_sum(features, grad_logits)
    from_classes = pair_scores(grad_logits, class_weight)

    def score_block(row_start):
        queries = lax.dynamic_slice_in_dim(gathered, row_start, BLK, 0)
        row_ids = row_start + jnp.arange(BLK, dtype=jnp.int32)
        query_labels = lax.dynamic_slice_in_dim(label_rows, row_start, BLK, 0)
        query_keep = lax.dynamic_slice_in_dim(keep_mask, row_start, BLK, 0)
        return (queries,) + row_terms(
            queries, row_ids, query_labels, query_keep, gathered, label_rows, keep_mask
        )

    zero_scalar = jnp.zeros((), jnp.float32)

    def visit_block(block_id, loop_state):
        key_grad, own_grad, contrast_sum = loop_state
        queries, scores, allowed, same_mask, logsum, pos_count, keep_float, anchor_loss = (
            score_block(own_start + block_id * BLK)
        )
        coefficient = coefficients(
            scores, allowed, same_mask, logsum[:, None], pos_count[:, None], keep_float[:, None]
        )
        row_grad = jnp.dot(coefficient, gathered, preferred_element_type=jnp.float32)
        own_grad = lax.dynamic_update_slice_in_dim(own_grad, row_grad, block_id * BLK, 0)
        key_grad = key_grad + column_sum(coefficient, queries)
        return (key_grad, own_grad, contrast_sum + jnp.sum(anchor_loss))

    start_state = (
        jnp.zeros((total_rows, emb_width), jnp.float32),
        jnp.zeros((slot_count, emb_width), jnp.float32),
        zero_scalar,
    )
    key_grad, own_grad, contrast_sum = lax.fori_loop(0, own_blocks, visit_block, start_state)
    grad_embedded = own_grad + lax.psum_scatter(key_grad, "group", scatter_dimension=0, tiled=True)
    radial = jnp.sum(unit_rows * grad_embedded, axis=1, keepdims=True)
    grad_projected = (grad_embedded - unit_rows * radial) / length
    proj_part = exact_column(picked.astype(jnp.float32), grad_projected)
    grad_picked = exact_pair(grad_projected, proj_weight.astype(jnp.float32))
    loss_parts = jnp.stack([jnp.sum(pixel_loss), contrast_sum])
    grad_proj, grad_class, loss_sums = lax.psum((proj_part, class_part, loss_parts), "group")
    scattered = jnp.zeros((pixel_count, channels), jnp.float32).at[pix_ids].add(grad_picked)
    grad_features = (from_classes + scattered).astype(jnp.bfloat16)
    valid_count = jnp.sum(keep_mask.astype(jnp.float32))
    losses = loss_sums / jnp.stack([jnp.float32(groups * pixel_count), valid_count])
    return (grad_features, grad_proj, grad_class, losses)


def solution(mesh):
    return jax.shard_map(
        per_device,
        mesh=mesh,
        in_specs=(
            P(("dp", "group"), None),
            P(),
            P("dp", None),
            P("dp"),
            P(("dp", "group"), None),
            P("dp", None),
            P(("dp", "group")),
        ),
        out_specs=(P(("dp", "group"), None), P("dp", None), P("dp", None), P("dp")),
        check_vma=False,
    )
```

profile of v0, /device:TPU:128, one launch (start us, length us, event | category | flops | bytes accessed | tf_op | source)
XLA Modules:
  0.0 394.0 jit_solution(9368211706606083540)
XLA Ops:
  7.3 0.8 compare_select_fusion
  8.1 0.7 copy-done
  8.8 2.0 gather_fusion
  10.8 0.4 multiply_reduce_fusion.1
  11.2 0.8 copy-done.1
  11.9 0.7 fusion.16
  12.8 0.6 broadcast_multiply_fusion
  13.5 63.4 %all-gather.2.cloned.1.call-done = bf16[8192,256]{0,1:T(8,128)(2,1)} async-done(((bf16[512,256]{0,1:T(8,128)(2,1)}), bf16[8192,256]{0,1:T(8,128)(2,1)}) %all-gather.2.cloned.1.call-update) | async-done | bytes 4194320 | tf_op jit(solution)/shard_map/all_gather | solution.py:86
  76.9 6.4 %copy.19 = bf16[8192,256]{1,0:T(8,128)(2,1)} copy(bf16[8192,256]{0,1:T(8,128)(2,1)} %all-gather.2.cloned.1.call-done) | data formatting | bytes 8388608 | tf_op jit(solution)/shard_map/while | solution.py:138
  83.3 3.8 broadcast_in_dim.19
  87.1 73.5 %while.16 = (s32[]{:T(128)}, f32[8192,256]{1,0:T(8,128)}, f32[512,256]{0,1:T(8,128)S(1)}, f32[]{:T(128)}, s32[]{:T(128)}, /*index=5*/s32[]{:T(128)}, pred[8192]{...) while((s32[]{:T(128)}, f32[8192,256]{1,0:T(8,128)}, ...), condition=%wide.region_9.10_spmd, body=%wide.region_4.9_spmd.sunk | while | flops 1650459520 | bytes 54990896 | solution.py:138
  87.8 0.1 dynamic_slice.35
  87.9 7.2 %select_reduce_fusion.4 = (f32[128]{0:T(128)S(1)}, f32[128]{0:T(128)S(1)}, f32[128]{0:T(128)S(1)}, f32[128,8192]{1,0:T(8,128)}) fusion(s32[8192]{0:T(1024)S(1)} %bitcast.35, s32[128]{0:T(128)S(1)} %dynamic_slice.35, s32[128]{0:T(128)S(1)} %iota_add_fusion.2, pred[8192]{0:T(1024)(128)(4,1)S(1)} %get-tuple-element.335, ...), kind=kOutput, calls=%fused_computation.9.clone.1 | convolution fusion | flops 549453440 | bytes 8497668 | tf_op jit(solution)/shard_map/while/body/dot_general | solution.py:15
  95.1 0.7 fusion.41
  95.9 7.1 %convolution_dynamic-update-slice_fusion.2 = f32[512,256]{0,1:T(8,128)S(1)} fusion(f32[512,256]{0,1:T(8,128)S(1)} %get-tuple-element.316, s32[]{:T(128)S(6)} %select_n.59, bf16[8192,256]{1,0:T(8,128)(2,1)} %get-tuple-element.338, f32[128,8192]{1,0:T(8,128)} %get-tuple-element.291, f32[128]{0:T(128)S(1)} %get-tuple-element.295, ...), kind=kOutput, calls=%fused_computation.14.clone.1 | convolution fusion | flops 549453824 | bytes 8563716 | tf_op jit(solution)/shard_map/while/body/dynamic_update_slice | solution.py:129
  103.0 7.7 %convolution_add_fusion.2 = f32[8192,256]{1,0:T(8,128)} fusion(f32[8192,256]{1,0:T(8,128)} %get-tuple-element.315, bf16[8192,256]{1,0:T(8,128)(2,1)} %get-tuple-element.338, s32[]{:T(128)S(6)} %select_n.58, f32[128,8192]{1,0:T(8,128)S(1)} %copy-done.15, f32[128]{0:T(128)S(1)} %get-tuple-element.295, f32[128]{0:T(128)S(1)} %get-tuple-element.296, ...), kind=kOutput, calls=%fused_computation.2.clone.1 | convolution fusion | flops 551550976 | bytes 21081092 | tf_op jit(solution)/shard_map/while/body/dot_general | solution.py:21
  112.1 0.1 dynamic_slice.35
  112.2 7.2 %select_reduce_fusion.4 = (f32[128]{0:T(128)S(1)}, f32[128]{0:T(128)S(1)}, f32[128]{0:T(128)S(1)}, f32[128,8192]{1,0:T(8,128)}) fusion(s32[8192]{0:T(1024)S(1)} %bitcast.35, s32[128]{0:T(128)S(1)} %dynamic_slice.35, s32[128]{0:T(128)S(1)} %iota_add_fusion.2, pred[8192]{0:T(1024)(128)(4,1)S(1)} %get-tuple-element.335, ...), kind=kOutput, calls=%fused_computation.9.clone.1 | convolution fusion | flops 549453440 | bytes 8497668 | tf_op jit(solution)/shard_map/while/body/dot_general | solution.py:15
  119.4 0.7 fusion.41
  120.2 7.1 %convolution_dynamic-update-slice_fusion.2 = f32[512,256]{0,1:T(8,128)S(1)} fusion(f32[512,256]{0,1:T(8,128)S(1)} %get-tuple-element.316, s32[]{:T(128)S(6)} %select_n.59, bf16[8192,256]{1,0:T(8,128)(2,1)} %get-tuple-element.338, f32[128,8192]{1,0:T(8,128)} %get-tuple-element.291, f32[128]{0:T(128)S(1)} %get-tuple-element.295, ...), kind=kOutput, calls=%fused_computation.14.clone.1 | convolution fusion | flops 549453824 | bytes 8563716 | tf_op jit(solution)/shard_map/while/body/dynamic_update_slice | solution.py:129
  127.3 7.7 %convolution_add_fusion.2 = f32[8192,256]{1,0:T(8,128)} fusion(f32[8192,256]{1,0:T(8,128)} %get-tuple-element.315, bf16[8192,256]{1,0:T(8,128)(2,1)} %get-tuple-element.338, s32[]{:T(128)S(6)} %select_n.58, f32[128,8192]{1,0:T(8,128)S(1)} %copy-done.15, f32[128]{0:T(128)S(1)} %get-tuple-element.295, f32[128]{0:T(128)S(1)} %get-tuple-element.296, ...), kind=kOutput, calls=%fused_computation.2.clone.1 | convolution fusion | flops 551550976 | bytes 21081092 | tf_op jit(solution)/shard_map/while/body/dot_general | solution.py:21
  136.4 0.1 dynamic_slice.35
  136.5 7.2 %select_reduce_fusion.4 = (f32[128]{0:T(128)S(1)}, f32[128]{0:T(128)S(1)}, f32[128]{0:T(128)S(1)}, f32[128,8192]{1,0:T(8,128)}) fusion(s32[8192]{0:T(1024)S(1)} %bitcast.35, s32[128]{0:T(128)S(1)} %dynamic_slice.35, s32[128]{0:T(128)S(1)} %iota_add_fusion.2, pred[8192]{0:T(1024)(128)(4,1)S(1)} %get-tuple-element.335, ...), kind=kOutput, calls=%fused_computation.9.clone.1 | convolution fusion | flops 549453440 | bytes 8497668 | tf_op jit(solution)/shard_map/while/body/dot_general | solution.py:15
  143.7 0.7 fusion.41
  144.5 7.1 %convolution_dynamic-update-slice_fusion.2 = f32[512,256]{0,1:T(8,128)S(1)} fusion(f32[512,256]{0,1:T(8,128)S(1)} %get-tuple-element.316, s32[]{:T(128)S(6)} %select_n.59, bf16[8192,256]{1,0:T(8,128)(2,1)} %get-tuple-element.338, f32[128,8192]{1,0:T(8,128)} %get-tuple-element.291, f32[128]{0:T(128)S(1)} %get-tuple-element.295, ...), kind=kOutput, calls=%fused_computation.14.clone.1 | convolution fusion | flops 549453824 | bytes 8563716 | tf_op jit(solution)/shard_map/while/body/dynamic_update_slice | solution.py:129
  151.6 7.7 %convolution_add_fusion.2 = f32[8192,256]{1,0:T(8,128)} fusion(f32[8192,256]{1,0:T(8,128)} %get-tuple-element.315, bf16[8192,256]{1,0:T(8,128)(2,1)} %get-tuple-element.338, s32[]{:T(128)S(6)} %select_n.58, f32[128,8192]{1,0:T(8,128)S(1)} %copy-done.15, f32[128]{0:T(128)S(1)} %get-tuple-element.295, f32[128]{0:T(128)S(1)} %get-tuple-element.296, ...), kind=kOutput, calls=%fused_computation.2.clone.1 | convolution fusion | flops 551550976 | bytes 21081092 | tf_op jit(solution)/shard_map/while/body/dot_general | solution.py:21
  160.7 9.1 %copy.20 = f32[8192,256]{0,1:T(8,128)} copy(f32[8192,256]{1,0:T(8,128)} %get-tuple-element.135) | data formatting | bytes 16777216 | tf_op jit(solution)/shard_map/while | solution.py:138
  169.8 0.2 all-reduce.3.cloned.1.call-start
  170.0 0.6 copy-done.6
  170.7 0.8 fusion.19
  171.5 0.3 select_reduce_fusion.2
  171.8 0.6 subtract_reduce_fusion
  172.4 1.2 convolution_bitcast_fusion
  173.6 109.0 %reduce-scatter.2.cloned.1.call-done = f32[512,256]{0,1:T(8,128)} async-done(((f32[8192,256]{0,1:T(8,128)}), f32[512,256]{0,1:T(8,128)}) %reduce-scatter.2.cloned.1.call-update) | async-done | bytes 524304 | tf_op jit(solution)/shard_map/reduce_scatter | solution.py:139
  282.6 1.5 multiply_reduce_fusion
  284.2 0.8 copy-done.5
  284.9 2.8 fusion.17
  287.8 2.7 fusion.14
  290.4 0.7 pad_maximum_fusion
  291.2 0.7 convert_reduce_fusion.1
  291.9 38.1 %psum.23 = f32[2]{0:T(128)S(1)} all-reduce(f32[2]{0:T(128)S(1)} %pad_maximum_fusion), channel_id=1, replica_groups=mesh['dp'=16,'group'=16] {'group'}, use_global_device_ids=true, to_apply=%region_17.18 | all-reduce | flops 2 | bytes 16 | tf_op jit(solution)/shard_map/psum | solution.py:145
  330.0 1.3 maximum_divide_fusion
  331.3 2.3 fusion.18
  333.6 7.8 %scatter_fusion = f32[2048,512]{1,0:T(8,128)} fusion(f32[2048,512]{1,0:T(8,128)} %fusion.14, s32[512]{0:T(512)} %bitcast.40, f32[512,512]{1,0:T(8,128)S(1)} %fusion.18), kind=kCustom, calls=%fused_computation.1 | custom fusion | flops 262144 | bytes 3147776 | tf_op jit(solution)/shard_map/scatter-add | solution.py:146
  341.3 3.8 convert_element_type.39
  345.1 38.6 %all-reduce.3.cloned.1.call-done = (f32[512,256]{1,0:T(8,128)}, f32[512,124]{0,1:T(8,128)}) async-done(((f32[512,256]{1,0:T(8,128)}, f32[512,124]{0,1:T(8,128)}), (f32[512,256]{1,0:T(8,128)}, f32[512,124]{0,1:T(8,128)})) %all-reduce.3.cloned.1.call-update) | async-done | bytes 778256 | tf_op jit(solution)/shard_map/psum | solution.py:145
  383.8 1.8 copy.22
  385.6 1.9 copy.55
  (52 shorter events, 0.6 us)
Async XLA Ops:
  7.2 1.6 copy-start
  7.2 3.6 copy-start.7
  7.2 5.6 %copy-start.14 = (s32[16]{0:T(128)S(1)}, s32[16]{0:T(128)}, u32[]{:S(2)}) copy-start(s32[16]{0:T(128)} %param.12) | copy-start | bytes 196
  7.2 6.3 %copy-start.4 = (s32[16,512]{1,0:T(8,128)S(1)}, s32[16,512]{1,0:T(8,128)}, u32[]{:S(2)}) copy-start(s32[16,512]{1,0:T(8,128)} %param.14) | copy-start | bytes 98308
  7.2 69.7 %all-gather.2.cloned.1.call-start = ((), (), s32[]{:S(2)}) async-start(), calls=%async_computation.1 | async-start | bytes 4456448 | tf_op jit(solution)/shard_map/all_gather | solution.py:86
  8.1 5.3 %copy-start.9 = (s32[512,1]{0,1:T(1,128)}, s32[512,1]{0,1:T(1,128)S(1)}, u32[]{:S(2)}) copy-start(s32[512,1]{0,1:T(1,128)S(1)} %compare_select_fusion) | copy-start | bytes 6148
  10.8 72.5 %copy-start.2 = (bf16[512,512]{1,0:T(8,128)(2,1)}, bf16[512,512]{1,0:T(8,128)(2,1)S(1)}, u32[]{:S(2)}) copy-start(bf16[512,512]{1,0:T(8,128)(2,1)S(1)} %gather_fusion) | copy-start | bytes 1572868
  11.1 0.8 copy-start.1
  11.2 2.2 copy-start.10
  12.7 269.9 %reduce-scatter.2.cloned.1.call-start = ((), (), s32[]{:S(2)}) async-start(), calls=%async_computation.2 | async-start | bytes 8912896 | tf_op jit(solution)/shard_map/reduce_scatter | solution.py:139
  13.4 69.9 %copy-start.11 = (s32[16]{0:T(128)}, s32[16]{0:T(128)S(1)}, u32[]{:S(2)}) copy-start(s32[16]{0:T(128)S(1)} %get-tuple-element.215) | copy-start | bytes 196
  95.9 7.2 %copy-start.15 = (f32[128,8192]{1,0:T(8,128)S(1)}, f32[128,8192]{1,0:T(8,128)}, u32[]{:S(2)}) copy-start(f32[128,8192]{1,0:T(8,128)} %get-tuple-element.291) | copy-start | bytes 12582916 | tf_op jit(solution)/shard_map/while
  120.2 7.2 %copy-start.15 = (f32[128,8192]{1,0:T(8,128)S(1)}, f32[128,8192]{1,0:T(8,128)}, u32[]{:S(2)}) copy-start(f32[128,8192]{1,0:T(8,128)} %get-tuple-element.291) | copy-start | bytes 12582916 | tf_op jit(solution)/shard_map/while
  144.5 7.2 %copy-start.15 = (f32[128,8192]{1,0:T(8,128)S(1)}, f32[128,8192]{1,0:T(8,128)}, u32[]{:S(2)}) copy-start(f32[128,8192]{1,0:T(8,128)} %get-tuple-element.291) | copy-start | bytes 12582916 | tf_op jit(solution)/shard_map/while
  160.6 9.1 %copy-start.3 = (f32[512,256]{0,1:T(8,128)}, f32[512,256]{0,1:T(8,128)S(1)}, u32[]{:S(2)}) copy-start(f32[512,256]{0,1:T(8,128)S(1)} %get-tuple-element.134) | copy-start | bytes 1572868
  169.8 0.9 copy-start.6
  169.8 1.7 copy-start.8
  169.8 214.0 %all-reduce.3.cloned.1.call-start = ((), (), s32[]{:S(2)}) async-start(), calls=%async_computation.3 | async-start | bytes 1572864 | tf_op jit(solution)/shard_map/psum | solution.py:145
  284.1 0.8 copy-start.5
  284.1 0.8 copy-start.13
  287.7 3.4 copy-start.12
Sparse Core Ops, SparseCore 0:
  12.8 64.0 all-gather.1
  169.9 112.6 reduce-scatter.1
  287.9 95.8 all-reduce.2
where the time goes:
time: 395 us; the launch traced here: 394 us
  waiting for transfers between devices  211 us (53%)
  matrix products  76.4 us (19%)
  blocking collectives  38.1 us (10%)
  local copies, waits for them, and re-layouts  28.1 us (7%)
  other arithmetic  21.3 us (5%)
  between operations  14 us (4%)
  loops' own time  4.7 us (1%)
    reduce_scatter x1, waiting for transfers between devices, per_device(): lax.psum_scatter(key_grad, 'group', scatter_dimension=0, tiled=True)  109 us
    all_gather x1, waiting for transfers between devices, per_device(): gathered = lax.all_gather(embedded, 'group', axis=0, tiled=True)  63.4 us
    psum x1, waiting for transfers between devices, per_device(): lax.psum((proj_part, class_part, loss_parts), 'group')  38.6 us
    psum x1, blocking collectives, per_device(): lax.psum((proj_part, class_part, loss_parts), 'group')  38.1 us
    dot_general x4, matrix products, pair_scores(): lax.dot_general(left, right, (((1,), (1,)), ((), ())), preferred_element_...  24.4 us
    dot_general x4, matrix products, column_sum(): lax.dot_general(left, right, (((0,), (0,)), ((), ())), preferred_element_...  24.3 us
    dynamic_update_slice x3, matrix products, visit_block(): lax.dynamic_update_slice_in_dim(own_grad, row_grad, block_id * BLK, 0)  21.4 us
    while x2, local copies, waits for them, and re-layouts, per_device(): lax.fori_loop(0, own_blocks, visit_block, start_state)  15.4 us
  transfers between devices with their start and end apart: 3, of which 3 were waited for; matrix products, arithmetic and copies ran while one was open for 6% of the time, Pallas kernels for 0%

commit v1 on v0

v1 whole, which is shorter than its diff:
```python
import functools

import jax
import jax.numpy as jnp
from jax import lax
from jax.experimental import pallas as pl
from jax.experimental.pallas import tpu as pltpu
from jax.sharding import PartitionSpec as P

BLK = 128
SOON = 4
UNIT = 16
PARTS = BLK // UNIT
TILE = 512
ROOM = 40
INV_TEMP = 10.0
EXP_SCALE = INV_TEMP * 1.4426950408889634
NORM_EPS = 1e-06
VMEM_BYTES = 63 * 1024 * 1024

NN = (((1,), (0,)), ((), ()))
NT = (((1,), (1,)), ((), ()))
TN = (((0,), (0,)), ((), ()))
F32 = jnp.float32
BF16 = jnp.bfloat16


def dot_f32(left, right, dims=NN):
    return lax.dot_general(left, right, dims, preferred_element_type=F32)


def split_bf16(value, count):
    parts = []
    for _ in range(count):
        parts.append(value.astype(BF16))
        value = value - parts[-1].astype(F32)
    return parts


def blocks_before(blocks_ref, image):
    total = jnp.int32(0)
    for group in range(blocks_ref.shape[0]):
        total = total + jnp.where(group < image, blocks_ref[group], 0)
    return total


def each_block(blocks_ref, visit):
    place = jnp.int32(0)
    for image in range(blocks_ref.shape[0]):
        count = blocks_ref[image]
        for block in range(4):
            pl.when(block < count)(functools.partial(visit, image, block, place + block))
        place = place + count


def fold_lanes(value):
    total = value[:, :BLK]
    for start in range(BLK, value.shape[1], BLK):
        total = total + value[:, start : start + BLK]
    return total


def column_of(row, height=BLK):
    return jnp.broadcast_to(row, (height, row.shape[1])).T[:, 0:1]


def project(picked, proj):
    projected = dot_f32(picked, proj)
    length = jnp.sqrt(jnp.sum(projected * projected, axis=1, keepdims=True) + NORM_EPS)
    return projected / length, length


def pick_kernel(
    blocks_ref, pix_ref, features_hbm, proj_ref, picked_ref, emb_ref, send_ref, features, sems
):
    slots = pix_ref.shape[1]
    step = features.shape[0] // sems.shape[0]
    copies = [
        pltpu.make_async_copy(
            features_hbm.at[pl.ds(part * step, step)],
            features.at[pl.ds(part * step, step)],
            sems.at[part],
        )
        for part in range(sems.shape[0])
    ]
    for copy in copies:
        copy.start()
    pix = column_of(pix_ref[...].astype(F32)).astype(jnp.int32)
    lanes = lax.broadcasted_iota(jnp.int32, (slots, step), 1)
    total = jnp.zeros((slots, features.shape[1]), F32)
    for part, copy in enumerate(copies):
        onehot = jnp.where(lanes == pix - part * step, 1.0, 0.0).astype(BF16)
        copy.wait()
        total = total + dot_f32(onehot, features[part * step : (part + 1) * step, :])
    picked = total.astype(BF16)
    picked_ref[...] = picked
    unit, _ = project(picked, proj_ref[...])
    emb_ref[...] = unit.astype(BF16)
    odd = lax.rem(blocks_before(blocks_ref, lax.axis_index("group")), 2)
    for half in range(2):
        first = half + odd - 2 * half * odd
        for part in range(PARTS):
            for pair in range(slots // BLK // 2):
                start = pl.multiple_of((2 * pair + first) * BLK + part * UNIT, UNIT)
                send_ref[half * PARTS + part, pair * UNIT : (pair + 1) * UNIT, :] = emb_ref[
                    pl.ds(start, UNIT), :
                ]


def label_kernel(
    blocks_ref, labels_ref, picked_ref, proj_ref,
    key_label_ref, info_ref, lanes_ref, unit_ref, length_ref, wide,
):
    unit, length = project(picked_ref[...], proj_ref[...])
    unit_ref[...] = unit
    length_ref[...] = jnp.broadcast_to(length, length_ref.shape)
    me = lax.axis_index("group")
    slots = labels_ref.shape[1]
    key_label_ref[...] = jnp.full_like(key_label_ref, -1.0)

    def place_labels(image, block, place):
        span = pl.ds(pl.multiple_of(place * BLK, BLK), BLK)
        part = labels_ref[image : image + 1, block * BLK : (block + 1) * BLK]
        key_label_ref[:, span] = part.astype(F32)

    each_block(blocks_ref, place_labels)
    class_ids = lax.broadcasted_iota(jnp.int32, (BLK, BLK), 0).astype(F32)
    counts = jnp.zeros((BLK, BLK), F32)
    for start in range(0, key_label_ref.shape[1], BLK):
        counts = counts + jnp.where(class_ids == key_label_ref[:, start : start + BLK], 1.0, 0.0)
    histogram = jnp.sum(counts, axis=1, keepdims=True)
    images = lax.broadcasted_iota(jnp.int32, labels_ref.shape, 0)
    own = jnp.where(images == me, labels_ref[...].astype(F32), 0.0)
    own = jnp.sum(own, axis=0, keepdims=True)
    own_ids = lax.broadcasted_iota(jnp.int32, (BLK, slots), 0).astype(F32)
    same = jnp.sum(jnp.where(own_ids == own, histogram, 0.0), axis=0, keepdims=True)
    slot_ids = lax.broadcasted_iota(jnp.int32, (1, slots), 1)
    keep = jnp.where(slot_ids < blocks_ref[me] * BLK, 1.0, 0.0)
    wide[...] = jnp.zeros_like(wide)
    wide[0:1, :] = keep
    wide[1:2, :] = own
    wide[2:3, :] = keep * (same - 1.0)
    lanes_ref[...] = wide[0:8, :]
    info_ref[...] = wide[...].T


def pack_kernel(first_unit, blocks_ref, recv_ref, rep_hbm, packed, sems):
    half = lax.div(lax.axis_index("group"), PARTS)
    packed[...] = jnp.zeros_like(packed)
    units = packed.shape[0] // UNIT

    def one_image(image, place):
        odd = lax.rem(place, 2)
        first = half + odd - 2 * half * odd
        for pair in range(2):
            block = 2 * pair + first
            unit = lax.div(place + block, 2) - first_unit

            @pl.when((block < blocks_ref[image]) & (unit >= 0) & (unit < units))
            def _():
                packed[pl.ds(pl.multiple_of(unit * UNIT, UNIT), UNIT), :] = recv_ref[
                    image, pair * UNIT : (pair + 1) * UNIT, :
                ]

        return place + blocks_ref[image]

    lax.fori_loop(0, blocks_ref.shape[0], one_image, jnp.int32(0))
    copies = [
        pltpu.make_async_copy(packed, rep_hbm.at[device], sems.at[device])
        for device in range(rep_hbm.shape[0])
    ]
    for copy in copies:
        copy.start()
    for copy in copies:
        copy.wait()


def skip_kernel(blocks_ref, out_hbm):
    pass


def load_keys(valid, keys_hbm, more_hbm, keys, sems):
    units = keys_hbm.shape[1]
    more = more_hbm.shape[1]

    def copies_of(which, source, start, count, place):
        return [
            pltpu.make_async_copy(
                source.at[device, pl.ds(start, count)],
                keys.at[pl.ds(place, count), device // PARTS, device % PARTS],
                sems.at[which, device],
            )
            for device in range(2 * PARTS)
        ]

    first = copies_of(0, keys_hbm, 0, SOON, 0)
    later = copies_of(1, keys_hbm, SOON, units - SOON, SOON)
    last = copies_of(2, more_hbm, 0, more, units)
    for copy in first + later:
        copy.start()

    @pl.when(valid > ROOM)
    def _():
        for copy in last:
            copy.start()
        for copy in last:
            copy.wait()

    def wait_first():
        for copy in first:
            copy.wait()

    def wait_later():
        for copy in later:
            copy.wait()

    return wait_first, wait_later


def each_tile(valid, waits, visit):
    wait_first, wait_later = waits
    wait_first()
    for tile in range(ROOM * BLK // TILE):
        if tile == SOON // 2:
            wait_later()
        visit(tile)

    def later(tile, carry):
        visit(tile)
        return carry

    per_tile = TILE // BLK
    lax.fori_loop(ROOM // per_tile, lax.div(valid + per_tile - 1, per_tile), later, 0)


def key_tile_of(keys, tile):
    return keys[pl.ds(2 * tile, 2)].reshape(TILE, keys.shape[-1])


def lanes_of(tile):
    start = tile * TILE
    return pl.ds(start if isinstance(start, int) else pl.multiple_of(start, TILE), TILE)


def not_own(rows, first_place, tile):
    row_ids = lax.broadcasted_iota(jnp.int32, (rows, TILE), 0)
    lane_ids = lax.broadcasted_iota(jnp.int32, (rows, TILE), 1)
    return lane_ids - row_ids != first_place * BLK - tile * TILE


def sums_kernel(
    blocks_ref, lanes_ref, own_ref, keys_hbm, more_hbm, grad_ref, acc_ref, send_ref,
    keys, sems,
):
    valid = blocks_before(blocks_ref, blocks_ref.shape[0])
    waits = load_keys(valid, keys_hbm, more_hbm, keys, sems)
    first_place = blocks_before(blocks_ref, lax.axis_index("group"))
    acc_ref[...] = jnp.zeros_like(acc_ref)
    grad_ref[...] = jnp.zeros_like(grad_ref)
    own = own_ref[...]
    lane_ids = lax.broadcasted_iota(jnp.int32, (1, TILE), 1)

    def visit(tile):
        key_tile = key_tile_of(keys, tile)
        in_use = jnp.where(lane_ids < valid * BLK - tile * TILE, 1.0, 0.0)
        weights = jnp.exp(dot_f32(own, key_tile, NT) * INV_TEMP) * in_use
        weights = jnp.where(not_own(own.shape[0], first_place, tile), weights, 0.0)
        acc_ref[...] += fold_lanes(weights)
        grad_ref[...] += dot_f32(weights.astype(BF16), key_tile)

    each_tile(valid, waits, visit)
    for block in range(own.shape[0] // BLK):
        rows = slice(block * BLK, (block + 1) * BLK)
        total = jnp.sum(acc_ref[rows, :].T, axis=0, keepdims=True)
        pos_count = lanes_ref[2:3, rows]
        scale = pos_count / jnp.maximum(pos_count, 1.0) / total
        for device in range(send_ref.shape[0]):
            send_ref[device, block : block + 1, :] = scale


def rows_kernel(
    blocks_ref, own_ref, info_ref, acc_ref, sum_grad_ref, key_label_ref, keys_hbm, more_hbm,
    grad_ref, same_ref, keys, by_class, squares, sems,
):
    valid = blocks_before(blocks_ref, blocks_ref.shape[0])
    waits = load_keys(valid, keys_hbm, more_hbm, keys, sems)
    class_ids = lax.broadcasted_iota(jnp.int32, (BLK, TILE), 0).astype(F32)
    by_class[...] = jnp.zeros_like(by_class)
    squares[...] = jnp.zeros_like(squares)

    def visit(tile):
        key_tile = key_tile_of(keys, tile)
        member = class_ids == key_label_ref[:, lanes_of(tile)]
        member = jnp.where(member, 1.0, 0.0).astype(BF16)
        by_class[...] += dot_f32(member, key_tile)
        wide = key_tile.astype(F32)
        for part in split_bf16(wide * wide, 2):
            squares[...] += dot_f32(member, part)

    each_tile(valid, waits, visit)
    counts = jnp.zeros((BLK, BLK), F32)
    for start in range(0, key_label_ref.shape[1], BLK):
        counts = counts + jnp.where(
            class_ids[:, :BLK] == key_label_ref[:, start : start + BLK], 1.0, 0.0
        )
    others = jnp.sum(counts, axis=1, keepdims=True) - 1.0
    sums = by_class[...]
    pair_sum = jnp.sum(sums * sums - squares[...], axis=1, keepdims=True)
    pair_sum = jnp.where(others > 0.5, pair_sum / jnp.maximum(others, 1.0), 0.0)
    same_ref[...] = jnp.broadcast_to(
        INV_TEMP * jnp.sum(pair_sum, axis=0, keepdims=True), same_ref.shape
    )
    keep = info_ref[:, 0:1]
    pos_count = info_ref[:, 2:3]
    lane_ids = lax.broadcasted_iota(jnp.int32, info_ref.shape, 1).astype(F32)
    member = jnp.where(lane_ids == info_ref[:, 1:2], 1.0, 0.0).astype(BF16)
    others = sum(dot_f32(member, part) for part in split_bf16(sums, 3))
    others = others - own_ref[...].astype(F32)
    pos_floor = jnp.maximum(pos_count, 1.0)
    total = jnp.sum(acc_ref[...], axis=1, keepdims=True)
    row_scale = keep * (pos_count / pos_floor) / total
    grad_ref[...] = row_scale * sum_grad_ref[...] - (2.0 * keep / pos_floor) * others


def keys_kernel(
    blocks_ref, own_ref, info_ref, scales_ref, same_ref, row_grad_hbm, unit_hbm, length_hbm,
    picked_hbm, class_hbm, keys_hbm, more_hbm, grad_ref, out_ref,
    keys, scale, acc, row_grad, unit, length, picked, sems, end_sems,
):
    valid = blocks_before(blocks_ref, blocks_ref.shape[0])
    waits = load_keys(valid, keys_hbm, more_hbm, keys, sems)
    late = [
        pltpu.make_async_copy(source, target, end_sems.at[i])
        for i, (source, target) in enumerate(
            [
                (row_grad_hbm, row_grad),
                (unit_hbm, unit),
                (length_hbm, length),
                (picked_hbm, picked),
                (class_hbm, out_ref.at[:, pl.ds(unit.shape[1], BLK)]),
            ]
        )
    ]
    for copy in late:
        copy.start()
    first_place = blocks_before(blocks_ref, lax.axis_index("group"))
    scale[...] = jnp.zeros_like(scale)

    def place_scales(image, block, place):
        span = pl.ds(pl.multiple_of(place * BLK, BLK), BLK)
        scale[:, span] = scales_ref[image, block : block + 1, :]

    each_block(blocks_ref, place_scales)
    acc[...] = jnp.zeros_like(acc)
    own = own_ref[...]

    def visit(tile):
        key_tile = key_tile_of(keys, tile)
        weights = jnp.exp(dot_f32(own, key_tile, NT) * INV_TEMP) * scale[:, lanes_of(tile)]
        weights = jnp.where(not_own(own.shape[0], first_place, tile), weights, 0.0)
        acc[...] += dot_f32(weights.astype(BF16), key_tile)

    each_tile(valid, waits, visit)
    for copy in late:
        copy.wait()
    grad = row_grad[...] + info_ref[:, 0:1] * acc[...]
    radial = jnp.sum(unit[...] * grad, axis=1, keepdims=True)
    grad = (grad - unit[...] * radial) / length[:, 0:1]
    grad_ref[...] = grad
    width = grad.shape[1]
    out_ref[:, :width] = sum(dot_f32(picked[...], part) for part in split_bf16(grad, 3))
    scales = scale[...]
    logs = jnp.where(scales > 0.0, -jnp.log(jnp.where(scales > 0.0, scales, 1.0)), 0.0)
    loss = jnp.sum(logs, axis=1, keepdims=True) - same_ref[...]
    last = (out_ref.shape[0], 1)
    out_ref[:, width + BLK - 1 :] = jnp.broadcast_to(loss, last)


def features_kernel(pix_ref, grad_ref, proj_ref, logits_ref, class_ref, out_ref):
    rows = out_ref.shape[0]
    slots = pix_ref.shape[1]
    ids = pl.program_id(0) * rows + lax.broadcasted_iota(jnp.int32, (rows, slots), 0)
    onehot = jnp.where(ids == pix_ref[...], 1.0, 0.0).astype(BF16)
    proj = proj_ref[...]
    total = dot_f32(logits_ref[...], class_ref[...], NT)
    for part in split_bf16(grad_ref[...], 2):
        total = total + dot_f32(dot_f32(onehot, part).astype(BF16), proj, NT)
    out_ref[...] = total.astype(BF16)


def add_kernel(classes, recv_ref, rep_hbm, total_ref, sems):
    total = recv_ref[0]
    for device in range(1, recv_ref.shape[0]):
        total = total + recv_ref[device]
    high, middle, low = split_bf16(total, 3)
    rows = lax.broadcasted_iota(jnp.int32, total.shape, 0)
    is_loss = lax.broadcasted_iota(jnp.int32, total.shape, 1) >= total.shape[1] - BLK + classes
    parts = jnp.where(rows == 1, middle.astype(F32), low.astype(F32))
    value = jnp.where(is_loss & (rows > 0), parts, high.astype(F32))
    total_ref[...] = value.astype(BF16)
    copies = [
        pltpu.make_async_copy(total_ref, rep_hbm.at[device], sems.at[device])
        for device in range(rep_hbm.shape[0])
    ]
    for copy in copies:
        copy.start()
    for copy in copies:
        copy.wait()


def end_kernel(pixels, blocks_ref, summed_ref, proj_ref, class_ref, losses_ref):
    width = proj_ref.shape[1]
    classes = class_ref.shape[1]
    summed = summed_ref[...].astype(F32)
    proj_ref[...] = summed[:, :width]
    class_ref[...] = summed[:, width : width + classes]
    groups = blocks_ref.shape[0]
    anchors = (blocks_before(blocks_ref, groups) * (groups * BLK)).astype(F32)
    top = summed[:8, width:]
    rows = lax.broadcasted_iota(jnp.int32, top.shape, 0)
    lanes = lax.broadcasted_iota(jnp.int32, top.shape, 1)
    pixel_loss = jnp.sum(jnp.where((rows < 3) & (lanes == classes), top, 0.0))
    contrast = jnp.sum(jnp.where((rows < 3) & (lanes == BLK - 1), top, 0.0))
    losses_ref[0] = pixel_loss / pixels
    losses_ref[1] = contrast / anchors


SMEM = pl.BlockSpec(memory_space=pltpu.SMEM)
VMEM = pl.BlockSpec()
ANY = pl.BlockSpec(memory_space=pl.ANY)


def shape_of(shape, dtype=F32):
    return jax.ShapeDtypeStruct(shape, dtype)


def call(kernel, name, ins, outs, out_specs=None, scratch=(), flops=0, exps=0):
    size = sum(a.size * a.dtype.itemsize for a, _ in ins)
    size += sum(o.size * o.dtype.itemsize for o in outs)
    return pl.pallas_call(
        kernel,
        name=name,
        out_shape=outs,
        in_specs=[s for _, s in ins],
        out_specs=out_specs or [VMEM] * len(outs),
        scratch_shapes=list(scratch),
        compiler_params=pltpu.CompilerParams(vmem_limit_bytes=VMEM_BYTES),
        cost_estimate=pl.CostEstimate(flops=flops, bytes_accessed=size, transcendentals=exps),
    )(*[a for a, _ in ins])


def exchange(value):
    return lax.all_to_all(value, "group", 0, 0, tiled=True)


def per_device(
    features, proj_weight, class_weight, anchor_blocks, anchor_pix, anchor_label, pixel_label
):
    groups = lax.axis_size("group")
    slots = anchor_pix.shape[1]
    pixels, channels = features.shape
    classes = class_weight.shape[1]
    width = proj_weight.shape[1]
    per_image = slots // BLK
    blocks = groups * per_image
    share = channels // groups
    valid = jnp.sum(anchor_blocks)

    picked, emb, send = call(
        pick_kernel, "pick_anchors",
        [(anchor_blocks, SMEM), (anchor_pix, VMEM), (features, ANY), (proj_weight, VMEM)],
        [shape_of((slots, channels), BF16), shape_of((slots, width), BF16),
         shape_of((groups, slots // groups, width), BF16)],
        None, [pltpu.VMEM(features.shape, BF16), pltpu.SemaphoreType.DMA((4,))],
        flops=2 * slots * channels * (pixels + width),
    )
    recv = exchange(send)

    def packed(first_unit, units):
        (rep,) = call(
            functools.partial(pack_kernel, first_unit), "pack_keys",
            [(anchor_blocks, SMEM), (recv, VMEM)],
            [shape_of((groups, units * UNIT, width), BF16)], [ANY],
            [pltpu.VMEM((units * UNIT, width), BF16), pltpu.SemaphoreType.DMA((groups,))],
        )
        return rep

    units, more_units = ROOM // 2, (blocks - ROOM) // 2

    def second_exchange():
        return exchange(packed(units, more_units))

    def no_exchange():
        shape = shape_of((groups, more_units * UNIT, width), BF16)
        return call(skip_kernel, "skip_keys", [(anchor_blocks, SMEM)], [shape], [ANY])[0]

    rep = packed(0, units)
    keys = exchange(rep).reshape(groups, units, UNIT, width)
    more = lax.cond(valid > ROOM, second_exchange, no_exchange)
    more = more.reshape(groups, more_units, UNIT, width)

    labels, late_features, _ = lax.optimization_barrier((anchor_label, features, rep))
    key_label, info, lanes, unit, length = call(
        label_kernel, "anchor_labels",
        [(anchor_blocks, SMEM), (labels, VMEM), (picked, VMEM), (proj_weight, VMEM)],
        [shape_of((1, blocks * BLK)), shape_of((slots, BLK)), shape_of((8, slots)),
         shape_of((slots, width)), shape_of((slots, BLK))],
        None, [pltpu.VMEM((BLK, slots), F32)],
    )
    logits = jnp.dot(late_features, class_weight, preferred_element_type=F32)
    top_logit = jnp.max(logits, axis=1, keepdims=True)
    logsum_class = jnp.log(jnp.sum(jnp.exp(logits - top_logit), axis=1, keepdims=True)) + top_logit
    label_ids = jnp.arange(classes, dtype=jnp.int32)
    onehot = (pixel_label[:, None] == label_ids[None, :]).astype(F32)
    pixel_loss = jnp.sum(logsum_class[:, 0] - jnp.sum(onehot * logits, axis=1))
    grad_logits = (jnp.exp(logits - logsum_class) - onehot).astype(BF16)
    class_part = dot_f32(late_features, grad_logits, TN)
    tail = jnp.broadcast_to(pixel_loss, (channels, BLK - classes))
    class_part = jnp.concatenate([class_part, tail], axis=1)
    key_scratch = pltpu.VMEM((blocks // 2, 2, PARTS, UNIT, width), BF16)
    key_sems = [pltpu.SemaphoreType.DMA((3, groups))]
    pairs = slots * ROOM * BLK
    sum_grad, acc, sums = call(
        sums_kernel, "anchor_sums",
        [(anchor_blocks, SMEM), (lanes, VMEM), (emb, VMEM), (keys, ANY), (more, ANY)],
        [shape_of((slots, width)), shape_of((slots, BLK)), shape_of((groups, per_image, BLK))],
        None, [key_scratch] + key_sems, flops=4 * pairs * width, exps=pairs,
    )
    scales = exchange(sums)
    row_grad, same = call(
        rows_kernel, "anchor_rows",
        [(anchor_blocks, SMEM), (emb, VMEM), (info, VMEM), (acc, VMEM), (sum_grad, VMEM),
         (key_label, VMEM), (keys, ANY), (more, ANY)],
        [shape_of((slots, width)), shape_of((1, 1))],
        None,
        [key_scratch, pltpu.VMEM((BLK, width), F32), pltpu.VMEM((BLK, width), F32)] + key_sems,
        flops=6 * ROOM * BLK * BLK * width,
    )
    grad_projected, part = call(
        keys_kernel, "anchor_keys",
        [(anchor_blocks, SMEM), (emb, VMEM), (info, VMEM), (scales, VMEM), (same, VMEM),
         (row_grad, ANY), (unit, ANY), (length, ANY), (picked.T, ANY), (class_part, ANY),
         (keys, ANY), (more, ANY)],
        [shape_of((slots, width)), shape_of((channels, width + BLK))],
        None,
        [key_scratch, pltpu.VMEM((1, blocks * BLK), F32), pltpu.VMEM((slots, width), F32),
         pltpu.VMEM((slots, width), F32), pltpu.VMEM((slots, width), F32),
         pltpu.VMEM((slots, BLK), F32), pltpu.VMEM((channels, slots), BF16)]
        + key_sems + [pltpu.SemaphoreType.DMA((5,))],
        flops=4 * pairs * width, exps=pairs,
    )

    received = exchange(part.reshape(groups, share, width + BLK))
    tile = pixels // 4
    (grad_features,) = pl.pallas_call(
        features_kernel,
        name="feature_grads",
        grid=(pixels // tile,),
        out_shape=[shape_of((pixels, channels), BF16)],
        in_specs=[
            pl.BlockSpec((1, slots), lambda i: (0, 0)),
            pl.BlockSpec((slots, width), lambda i: (0, 0)),
            pl.BlockSpec((channels, width), lambda i: (0, 0)),
            pl.BlockSpec((tile, classes), lambda i: (i, 0)),
            pl.BlockSpec((channels, classes), lambda i: (0, 0)),
        ],
        out_specs=[pl.BlockSpec((tile, channels), lambda i: (i, 0))],
        compiler_params=pltpu.CompilerParams(vmem_limit_bytes=VMEM_BYTES),
        cost_estimate=pl.CostEstimate(
            flops=2 * pixels * (2 * slots * width + 2 * width * channels + classes * channels),
            bytes_accessed=4 * pixels * channels,
            transcendentals=0,
        ),
    )(anchor_pix, grad_projected, proj_weight, grad_logits, class_weight)
    (part_rep,) = call(
        functools.partial(add_kernel, classes), "add_shares", [(received, VMEM)],
        [shape_of(received.shape, BF16)], [ANY],
        [pltpu.VMEM(received.shape[1:], BF16), pltpu.SemaphoreType.DMA((groups,))],
    )
    summed = exchange(part_rep).reshape(channels, width + BLK)
    grad_proj, grad_class, losses = call(
        functools.partial(end_kernel, float(groups * pixels)), "outputs",
        [(anchor_blocks, SMEM), (summed, VMEM)],
        [shape_of((channels, width)), shape_of((channels, classes)), shape_of((2,))],
        [VMEM, VMEM, SMEM],
    )
    return (grad_features, grad_proj, grad_class, losses)


def solution(mesh):
    return jax.shard_map(
        per_device,
        mesh=mesh,
        in_specs=(
            P(("dp", "group"), None),
            P(),
            P("dp", None),
            P("dp"),
            P(("dp", "group"), None),
            P("dp", None),
            P(("dp", "group")),
        ),
        out_specs=(P(("dp", "group"), None), P("dp", None), P("dp", None), P("dp")),
        check_vma=False,
    )
```

time: 395 us -> 128 us (0.32)
  waiting for transfers between devices: 211 us -> 34.1 us
  matrix products: 76.4 us -> 3.17 us
  Pallas kernels: 0 us -> 43.5 us
  local copies, waits for them, and re-layouts: 28.1 us -> 4.27 us
  blocking collectives: 38.1 us -> 17.6 us
  starting transfers between devices: 0.3 us -> 19.5 us
  other arithmetic: 21.3 us -> 2.74 us
  between operations: 14 us -> 1.65 us
  loops' own time: 4.7 us -> 0.01 us
    reduce_scatter x1 -> x0, waiting for transfers between devices: 109 us -> none  [per_device(): lax.psum_scatter(key_grad, 'group', scatter_dimension=0, tiled=True)]
    all_gather x1 -> x0, waiting for transfers between devices: 63.4 us -> none  [per_device(): gathered = lax.all_gather(embedded, 'group', axis=0, tiled=True)]
    dot_general x12 -> x2, matrix products: 54.9 us -> 3.17 us  [the longest x1 2.43 us: per_device(): logits = jnp.dot(late_features, class_weight, preferred_element_type=F32)]
    pallas_call x0 -> x10, Pallas kernels: none -> 43.5 us  [the longest x9 37 us: call(): pl.pallas_call(kernel, name=name, out_shape=outs, in_specs=[s for _, s in...]
    psum x1 -> x0, waiting for transfers between devices: 38.6 us -> none  [per_device(): lax.psum((proj_part, class_part, loss_parts), 'group')]
    psum x1 -> x0, blocking collectives: 38.1 us -> none  [per_device(): lax.psum((proj_part, class_part, loss_parts), 'group')]
    all_to_all x0 -> x4, waiting for transfers between devices: none -> 34.1 us  [exchange(): return lax.all_to_all(value, 'group', 0, 0, tiled=True)]
    dynamic_update_slice x3 -> x0, matrix products: 21.4 us -> none  [visit_block(): lax.dynamic_update_slice_in_dim(own_grad, row_grad, block_id * BLK, 0)]
  transfers between devices with their start and end apart: 3 -> 4, of which waited for: 3 -> 4; matrix products, arithmetic and copies ran while one was open for 6% -> 7% of each run, Pallas kernels for 0% -> 13%
where the time goes in v1:
time: 128 us; the launch traced here: 127 us
  Pallas kernels  43.5 us (34%)
  waiting for transfers between devices  34.1 us (27%)
  starting transfers between devices  19.5 us (15%)
  blocking collectives  17.6 us (14%)
  local copies, waits for them, and re-layouts  4.27 us (3%)
  matrix products  3.17 us (2%)
  other arithmetic  2.74 us (2%)
  between operations  1.65 us (1%)
    pallas_call x9, Pallas kernels, call(): pl.pallas_call(kernel, name=name, out_shape=outs, in_specs=[s for _, s in...  37 us
    all_to_all x4, waiting for transfers between devices, exchange(): return lax.all_to_all(value, 'group', 0, 0, tiled=True)  34.1 us
    all_to_all x4, starting transfers between devices, exchange(): return lax.all_to_all(value, 'group', 0, 0, tiled=True)  19.5 us
    all_to_all x1, blocking collectives, exchange(): return lax.all_to_all(value, 'group', 0, 0, tiled=True)  17.6 us
    pallas_call x1, Pallas kernels, per_device(): pl.pallas_call(features_kernel, name='feature_grads', grid=(pixels // til...  6.5 us
  transfers between devices with their start and end apart: 4, of which 4 were waited for; matrix products, arithmetic and copies ran while one was open for 7% of the time, Pallas kernels for 13%

profile of v1, /device:TPU:128, one launch (start us, length us, event | category | flops | bytes accessed | tf_op | source)
XLA Modules:
  0.0 126.6 jit_solution(13638507474794261259)
XLA Ops:
  0.6 0.0 copy-start.7
  0.6 5.0 %pick_anchors.1 = (bf16[512,512]{1,0:T(8,128)(2,1)}, bf16[512,256]{1,0:T(8,128)(2,1)}, bf16[16,32,256]{2,1,0:T(8,128)(2,1)}) custom-call(s32[16]{0:T(128)} %blocks_ref.14, s32[1,512]{1,0:T(1,128)} %pix_ref.3, bf16[2048,512]{1,0:T(8,128)(2,1)} %features_hbm.1, bf16[512,256]{1,0:T(8,128)(2,1)} %proj_ref.5), custom_call_target="tpu_custom_call" | custom-call | flops 1207959552 | bytes 3409984 | tf_op jit(solution)/shard_map/pick_anchors/pallas_call | solution.py:440
  5.7 7.1 %all-to-all-start.1 = ((bf16[16,32,256]{2,1,0:T(8,128)(2,1)}), bf16[16,32,256]{2,1,0:T(8,128)(2,1)S(1)}, u32[]{:S(2)}, u32[]{:S(2)}) async-start(bf16[16,32,256]{2,1,0:T(8,128)(2,1)} %get-tuple-element.36), calls=%async_computation.1 | async-start | bytes 524288 | tf_op jit(solution)/shard_map/all_to_all | solution.py:453
  12.8 0.0 copy-done.7
  12.8 0.6 reduce_sum.36
  14.0 7.2 %all-to-all-done.1.recv_ref = bf16[16,32,256]{2,1,0:T(8,128)(2,1)S(1)} async-done(((bf16[16,32,256]{2,1,0:T(8,128)(2,1)}), bf16[16,32,256]{2,1,0:T(8,128)(2,1)S(1)}, u32[]{:S(2)}, u32[]{:S(2)}) %all-to-all-start.1) | async-done | bytes 262176 | tf_op jit(solution)/shard_map/all_to_all | solution.py:453
  21.3 0.5 conditional.1
  21.3 0.5 skip_keys.1
  21.8 2.7 %pack_keys.3 = bf16[16,320,256]{2,1,0:T(8,128)(2,1)} custom-call(s32[16]{0:T(128)S(1)} %copy-done.7, bf16[16,32,256]{2,1,0:T(8,128)(2,1)S(1)} %all-to-all-done.1.recv_ref), custom_call_target="tpu_custom_call" | custom-call | bytes 2883648 | tf_op jit(solution)/shard_map/pack_keys/pallas_call | solution.py:440
  24.5 0.0 copy-start.2
  24.5 0.0 copy-start.4
  24.5 4.6 %all-to-all-start.2 = ((bf16[16,320,256]{2,1,0:T(8,128)(2,1)}), bf16[16,320,256]{2,1,0:T(8,128)(2,1)}, u32[]{:S(2)}, u32[]{:S(2)}) async-start(bf16[16,320,256]{2,1,0:T(8,128)(2,1)} %pack_keys.3), calls=%async_computation.2 | async-start | bytes 5242880 | tf_op jit(solution)/shard_map/all_to_all | solution.py:453
  29.1 0.0 copy-done.2
  29.1 1.0 copy.11
  30.1 3.4 %anchor_labels.1 = (f32[1,8192]{1,0:T(1,128)}, f32[512,128]{1,0:T(8,128)}, f32[8,512]{1,0:T(8,128)}, f32[512,256]{1,0:T(8,128)}, f32[512,128]{1,0:T(8,128)}) custom-call(s32[16]{0:T(128)S(1)} %copy-done.7, s32[16,512]{1,0:T(8,128)} %labels_ref, bf16[512,512]{1,0:T(8,128)(2,1)} %get-tuple-element.38.picked_ref, bf16[512,256]{1,0:T(8,128)(2,1)} %proj_ref.5), custom_call_target="tpu_custom_call" | custom-call | bytes 1916992 | tf_op jit(solution)/shard_map/anchor_labels/pallas_call | solution.py:440
  33.5 0.0 copy-done.4
  33.5 2.4 %fusion = (f32[2048]{0:T(1024)S(1)}, f32[2048,124]{0,1:T(8,128)S(1)}) fusion(bf16[2048,512]{1,0:T(8,128)(2,1)} %features_hbm.1, bf16[512,124]{1,0:T(8,128)(2,1)S(1)} %copy-done.4), kind=kOutput, calls=%fused_computation.6 | convolution fusion | flops 260298752 | bytes 3248128 | tf_op jit(solution)/shard_map/dot_general | solution.py:510
  35.9 0.0 copy-start.5
  36.0 0.4 copy.12
  36.3 0.0 copy-start
  36.3 0.2 exponential_reduce_fusion
  36.5 0.1 copy-done.5
  36.6 0.6 select_reduce_fusion
  37.3 0.6 subtract_reduce_fusion
  37.9 0.7 subtract_convert_fusion.logits_ref
  38.6 0.0 copy-done
  38.6 0.0 copy-start.1
  38.6 0.7 fusion.1
  39.4 1.4 %concatenate.3.class_hbm = f32[512,128]{1,0:T(8,128)} pad(f32[512,124]{1,0:T(8,128)S(1)} %fusion.1, f32[]{:T(128)} %get-tuple-element.55), padding=0_0x0_4 | pad | bytes 516100 | tf_op jit(solution)/shard_map/concatenate | solution.py:519
  40.8 23.3 %all-to-all-done.2 = bf16[16,320,256]{2,1,0:T(8,128)(2,1)} async-done(((bf16[16,320,256]{2,1,0:T(8,128)(2,1)}), bf16[16,320,256]{2,1,0:T(8,128)(2,1)}, u32[]{:S(2)}, u32[]{:S(2)}) %all-to-all-start.2) | async-done | bytes 2621472 | tf_op jit(solution)/shard_map/all_to_all | solution.py:453
  64.0 6.6 %anchor_sums.1 = (f32[512,256]{1,0:T(8,128)}, f32[512,128]{1,0:T(8,128)}, f32[16,4,128]{2,1,0:T(4,128)}) custom-call(s32[16]{0:T(128)S(1)} %copy-done.7, f32[8,512]{1,0:T(8,128)} %get-tuple-element.40.lanes_ref, bf16[512,256]{1,0:T(8,128)(2,1)} %get-tuple-element.35.own_ref, bf16[16,20,16,256]{3,2,1,0:T(8,128)(2,1)} %bitcast.2.keys_hbm, ...), custom_call_target="tpu_custom_call" | custom-call | flops 2684354560 | bytes 5292096 | tf_op jit(solution)/shard_map/anchor_sums/pallas_call | solution.py:440
  70.6 0.0 copy-done.1
  70.7 4.2 %all-to-all-start.3 = ((f32[16,4,128]{2,1,0:T(4,128)}), f32[16,4,128]{2,1,0:T(4,128)S(1)}, u32[]{:S(2)}, u32[]{:S(2)}) async-start(f32[16,4,128]{2,1,0:T(4,128)} %get-tuple-element.41), calls=%async_computation.3 | async-start | bytes 65536 | tf_op jit(solution)/shard_map/all_to_all | solution.py:453
  74.9 6.6 %anchor_rows.1 = (f32[512,256]{1,0:T(8,128)}, f32[1,1]{1,0:T(1,128)}) custom-call(s32[16]{0:T(128)S(1)} %copy-done.7, bf16[512,256]{1,0:T(8,128)(2,1)} %get-tuple-element.35.own_ref, f32[512,128]{1,0:T(8,128)} %get-tuple-element.39.info_ref, f32[512,128]{1,0:T(8,128)} %get-tuple-element.42.acc_ref, f32[512,256]{1,0:T(8,128)} %get-tuple-element.43.sum_grad_ref, ...), custom_call_target="tpu_custom_call" | custom-call | flops 1006632960 | bytes 6062148 | tf_op jit(solution)/shard_map/anchor_rows/pallas_call | solution.py:440
  81.4 1.0 all-to-all-done.3.scales_ref
  82.5 0.0 copy-start.6
  82.5 0.6 copy-done.6
  83.1 8.2 %anchor_keys.1 = (f32[512,256]{1,0:T(8,128)}, f32[512,384]{1,0:T(8,128)}) custom-call(s32[16]{0:T(128)S(1)} %copy-done.7, bf16[512,256]{1,0:T(8,128)(2,1)} %get-tuple-element.35.own_ref, f32[512,128]{1,0:T(8,128)} %get-tuple-element.39.info_ref, f32[16,4,128]{2,1,0:T(4,128)} %copy-done.6, f32[1,1]{1,0:T(1,128)} %get-tuple-element.45.same_ref, ...), custom_call_target="tpu_custom_call" | custom-call | flops 2684354560 | bytes 8159300 | tf_op jit(solution)/shard_map/anchor_keys/pallas_call | solution.py:440
  91.3 17.6 %all_to_all.30.recv_ref = f32[16,32,384]{2,1,0:T(8,128)} all-to-all(f32[16,32,384]{2,1,0:T(8,128)} %bitcast.13), channel_id=1, replica_groups=mesh['dp'=16,'group'=16] {'group'}, dimensions={0} | all-to-all | bytes 1572864 | tf_op jit(solution)/shard_map/all_to_all | solution.py:453
  108.9 2.1 %add_shares.1 = bf16[16,32,384]{2,1,0:T(8,128)(2,1)} custom-call(f32[16,32,384]{2,1,0:T(8,128)} %all_to_all.30.recv_ref), custom_call_target="tpu_custom_call" | custom-call | bytes 1179648 | tf_op jit(solution)/shard_map/add_shares/pallas_call | solution.py:440
  111.0 3.6 %all-to-all-start.5 = ((bf16[16,32,384]{2,1,0:T(8,128)(2,1)}), bf16[16,32,384]{2,1,0:T(8,128)(2,1)S(1)}, u32[]{:S(2)}, u32[]{:S(2)}) async-start(bf16[16,32,384]{2,1,0:T(8,128)(2,1)} %add_shares.1), calls=%async_computation.5 | async-start | bytes 786432 | tf_op jit(solution)/shard_map/all_to_all | solution.py:453
  114.7 6.5 %feature_grads.1 = bf16[2048,512]{1,0:T(8,128)(2,1)} custom-call(s32[1,512]{1,0:T(1,128)} %pix_ref.3, f32[512,256]{1,0:T(8,128)} %get-tuple-element.50.grad_ref, bf16[512,256]{1,0:T(8,128)(2,1)} %proj_ref.5, bf16[2048,124]{1,0:T(8,128)(2,1)} %copy-done.1, bf16[512,124]{1,0:T(8,128)(2,1)} %class_ref.1), custom_call_target="tpu_custom_call" | custom-call | flops 2407530496 | bytes 4194304 | tf_op jit(solution)/shard_map/feature_grads/pallas_call | solution.py:555
  121.2 2.6 %all-to-all-done.5 = bf16[16,32,384]{2,1,0:T(8,128)(2,1)S(1)} async-done(((bf16[16,32,384]{2,1,0:T(8,128)(2,1)}), bf16[16,32,384]{2,1,0:T(8,128)(2,1)S(1)}, u32[]{:S(2)}, u32[]{:S(2)}) %all-to-all-start.5) | async-done | bytes 393248 | tf_op jit(solution)/shard_map/all_to_all | solution.py:453
  123.8 0.0 copy-start.3
  123.8 0.7 copy-done.3
  124.5 1.9 %outputs.1 = (f32[512,256]{1,0:T(8,128)}, f32[512,124]{1,0:T(8,128)}, f32[2]{0:T(128)}) custom-call(s32[16]{0:T(128)S(1)} %copy-done.7, bf16[512,384]{1,0:T(8,128)(2,1)} %bitcast.12), custom_call_target="tpu_custom_call" | custom-call | bytes 1171528 | tf_op jit(solution)/shard_map/outputs/pallas_call | solution.py:440
Async XLA Ops:
  0.6 12.1 %copy-start.7 = (s32[16]{0:T(128)S(1)}, s32[16]{0:T(128)}, u32[]{:S(2)}) copy-start(s32[16]{0:T(128)} %blocks_ref.14) | copy-start | bytes 196
  5.7 15.6 %all-to-all-start.1 = ((bf16[16,32,256]{2,1,0:T(8,128)(2,1)}), bf16[16,32,256]{2,1,0:T(8,128)(2,1)S(1)}, u32[]{:S(2)}, u32[]{:S(2)}) async-start(bf16[16,32,256]{2,1,0:T(8,128)(2,1)} %get-tuple-element.36), calls=%async_computation.1 | async-start | bytes 524288 | tf_op jit(solution)/shard_map/all_to_all | solution.py:453
  24.5 4.6 %copy-start.2 = (bf16[512,512]{1,0:T(8,128)(2,1)S(1)}, bf16[512,512]{1,0:T(8,128)(2,1)}, u32[]{:S(2)}) copy-start(bf16[512,512]{1,0:T(8,128)(2,1)} %get-tuple-element.38.picked_ref) | copy-start | bytes 1572868
  24.5 9.0 %copy-start.4 = (bf16[512,124]{1,0:T(8,128)(2,1)S(1)}, bf16[512,124]{1,0:T(8,128)(2,1)}, u32[]{:S(2)}) copy-start(bf16[512,124]{1,0:T(8,128)(2,1)} %class_ref.1) | copy-start | bytes 380932
  24.5 39.5 %all-to-all-start.2 = ((bf16[16,320,256]{2,1,0:T(8,128)(2,1)}), bf16[16,320,256]{2,1,0:T(8,128)(2,1)}, u32[]{:S(2)}, u32[]{:S(2)}) async-start(bf16[16,320,256]{2,1,0:T(8,128)(2,1)} %pack_keys.3), calls=%async_computation.2 | async-start | bytes 5242880 | tf_op jit(solution)/shard_map/all_to_all | solution.py:453
  35.9 0.7 copy-start.5
  36.3 2.3 %copy-start = (bf16[2048,512]{1,0:T(8,128)(2,1)S(1)}, bf16[2048,512]{1,0:T(8,128)(2,1)}, u32[]{:S(2)}) copy-start(bf16[2048,512]{1,0:T(8,128)(2,1)} %features_hbm.1) | copy-start | bytes 6291460
  38.6 32.0 %copy-start.1 = (bf16[2048,124]{1,0:T(8,128)(2,1)}, bf16[2048,124]{1,0:T(8,128)(2,1)S(1)}, u32[]{:S(2)}) copy-start(bf16[2048,124]{1,0:T(8,128)(2,1)S(1)} %subtract_convert_fusion.logits_ref) | copy-start | bytes 1523716
  70.7 11.8 %all-to-all-start.3 = ((f32[16,4,128]{2,1,0:T(4,128)}), f32[16,4,128]{2,1,0:T(4,128)S(1)}, u32[]{:S(2)}, u32[]{:S(2)}) async-start(f32[16,4,128]{2,1,0:T(4,128)} %get-tuple-element.41), calls=%async_computation.3 | async-start | bytes 65536 | tf_op jit(solution)/shard_map/all_to_all | solution.py:453
  82.5 0.6 copy-start.6
  111.0 12.8 %all-to-all-start.5 = ((bf16[16,32,384]{2,1,0:T(8,128)(2,1)}), bf16[16,32,384]{2,1,0:T(8,128)(2,1)S(1)}, u32[]{:S(2)}, u32[]{:S(2)}) async-start(bf16[16,32,384]{2,1,0:T(8,128)(2,1)} %add_shares.1), calls=%async_computation.5 | async-start | bytes 786432 | tf_op jit(solution)/shard_map/all_to_all | solution.py:453
  123.8 0.7 copy-start.3

commit v2 on v1

--- a/solution.py
+++ b/solution.py
@@ -8,7 +8,7 @@
 from jax.sharding import PartitionSpec as P
 
 BLK = 128
-SOON = 4
+SOON = (0, 2, 8)
 UNIT = 16
 PARTS = BLK // UNIT
 TILE = 512
@@ -17,6 +17,9 @@
 EXP_SCALE = INV_TEMP * 1.4426950408889634
 NORM_EPS = 1e-06
 VMEM_BYTES = 63 * 1024 * 1024
+MID_BYTES = 40 * 1024 * 1024
+LABEL_BYTES = 63 * 1024 * 1024
+SMALL_BYTES = 16 * 1024 * 1024
 
 NN = (((1,), (0,)), ((), ()))
 NT = (((1,), (1,)), ((), ()))
@@ -70,9 +73,7 @@
     return projected / length, length
 
 
-def pick_kernel(
-    blocks_ref, pix_ref, features_hbm, proj_ref, picked_ref, emb_ref, send_ref, features, sems
-):
+def pick(pix_ref, features_hbm, features, sems, beside):
     slots = pix_ref.shape[1]
     step = features.shape[0] // sems.shape[0]
     copies = [
@@ -85,6 +86,7 @@
     ]
     for copy in copies:
         copy.start()
+    beside()
     pix = column_of(pix_ref[...].astype(F32)).astype(jnp.int32)
     lanes = lax.broadcasted_iota(jnp.int32, (slots, step), 1)
     total = jnp.zeros((slots, features.shape[1]), F32)
@@ -92,8 +94,14 @@
         onehot = jnp.where(lanes == pix - part * step, 1.0, 0.0).astype(BF16)
         copy.wait()
         total = total + dot_f32(onehot, features[part * step : (part + 1) * step, :])
-    picked = total.astype(BF16)
-    picked_ref[...] = picked
+    return total
+
+
+def pick_kernel(
+    blocks_ref, pix_ref, features_hbm, proj_ref, emb_ref, send_ref, features, sems
+):
+    slots = pix_ref.shape[1]
+    picked = pick(pix_ref, features_hbm, features, sems, lambda: None).astype(BF16)
     unit, _ = project(picked, proj_ref[...])
     emb_ref[...] = unit.astype(BF16)
     odd = lax.rem(blocks_before(blocks_ref, lax.axis_index("group")), 2)
@@ -108,12 +116,20 @@
 
 
 def label_kernel(
-    blocks_ref, labels_ref, picked_ref, proj_ref,
-    key_label_ref, info_ref, lanes_ref, unit_ref, length_ref, wide,
+    blocks_ref, labels_ref, pix_ref, features_hbm, proj_ref,
+    key_label_ref, info_ref, lanes_ref, unit_ref, scale_ref, picked_ref, wide, features, sems,
 ):
-    unit, length = project(picked_ref[...], proj_ref[...])
+    def labels():
+        label_terms(blocks_ref, labels_ref, key_label_ref, info_ref, lanes_ref, wide)
+
+    picked = pick(pix_ref, features_hbm, features, sems, labels)
+    picked_ref[...] = picked.T.astype(BF16)
+    unit, length = project(picked.astype(BF16), proj_ref[...])
     unit_ref[...] = unit
-    length_ref[...] = jnp.broadcast_to(length, length_ref.shape)
+    scale_ref[...] = jnp.broadcast_to(info_ref[:, 0:1] / length, scale_ref.shape)
+
+
+def label_terms(blocks_ref, labels_ref, key_label_ref, info_ref, lanes_ref, wide):
     me = lax.axis_index("group")
     slots = labels_ref.shape[1]
     key_label_ref[...] = jnp.full_like(key_label_ref, -1.0)
@@ -193,11 +209,14 @@
             for device in range(2 * PARTS)
         ]
 
-    first = copies_of(0, keys_hbm, 0, SOON, 0)
-    later = copies_of(1, keys_hbm, SOON, units - SOON, SOON)
-    last = copies_of(2, more_hbm, 0, more, units)
-    for copy in first + later:
-        copy.start()
+    starts = [start for start in SOON if start < units]
+    waits = {}
+    for which, (start, end) in enumerate(zip(starts, starts[1:] + [units])):
+        copies = copies_of(which, keys_hbm, start, end - start, start)
+        for copy in copies:
+            copy.start()
+        waits[start // 2] = copies
+    last = copies_of(len(SOON), more_hbm, 0, more, units)
 
     @pl.when(valid > ROOM)
     def _():
@@ -206,24 +225,17 @@
         for copy in last:
             copy.wait()
 
-    def wait_first():
-        for copy in first:
+    return waits
+
+
+def each_tile(valid, waits, visit):
+    for tile in range(ROOM * BLK // TILE):
+        for copy in waits.get(tile, ()):
             copy.wait()
-
-    def wait_later():
-        for copy in later:
-            copy.wait()
-
-    return wait_first, wait_later
-
-
-def each_tile(valid, waits, visit):
-    wait_first, wait_later = waits
-    wait_first()
-    for tile in range(ROOM * BLK // TILE):
-        if tile == SOON // 2:
-            wait_later()
-        visit(tile)
+        if (tile + 1) * TILE < ROOM * BLK:
+            visit(tile)
+        else:
+            pl.when(valid > tile * (TILE // BLK))(functools.partial(visit, tile))
 
     def later(tile, carry):
         visit(tile)
@@ -280,51 +292,38 @@
 
 def rows_kernel(
     blocks_ref, own_ref, info_ref, acc_ref, sum_grad_ref, key_label_ref, keys_hbm, more_hbm,
-    grad_ref, same_ref, keys, by_class, squares, sems,
+    grad_ref, loss_ref, keys, by_class, sems,
 ):
     valid = blocks_before(blocks_ref, blocks_ref.shape[0])
     waits = load_keys(valid, keys_hbm, more_hbm, keys, sems)
     class_ids = lax.broadcasted_iota(jnp.int32, (BLK, TILE), 0).astype(F32)
     by_class[...] = jnp.zeros_like(by_class)
-    squares[...] = jnp.zeros_like(squares)
 
     def visit(tile):
-        key_tile = key_tile_of(keys, tile)
         member = class_ids == key_label_ref[:, lanes_of(tile)]
         member = jnp.where(member, 1.0, 0.0).astype(BF16)
-        by_class[...] += dot_f32(member, key_tile)
-        wide = key_tile.astype(F32)
-        for part in split_bf16(wide * wide, 2):
-            squares[...] += dot_f32(member, part)
+        by_class[...] += dot_f32(member, key_tile_of(keys, tile))
 
     each_tile(valid, waits, visit)
-    counts = jnp.zeros((BLK, BLK), F32)
-    for start in range(0, key_label_ref.shape[1], BLK):
-        counts = counts + jnp.where(
-            class_ids[:, :BLK] == key_label_ref[:, start : start + BLK], 1.0, 0.0
-        )
-    others = jnp.sum(counts, axis=1, keepdims=True) - 1.0
-    sums = by_class[...]
-    pair_sum = jnp.sum(sums * sums - squares[...], axis=1, keepdims=True)
-    pair_sum = jnp.where(others > 0.5, pair_sum / jnp.maximum(others, 1.0), 0.0)
-    same_ref[...] = jnp.broadcast_to(
-        INV_TEMP * jnp.sum(pair_sum, axis=0, keepdims=True), same_ref.shape
-    )
     keep = info_ref[:, 0:1]
     pos_count = info_ref[:, 2:3]
     lane_ids = lax.broadcasted_iota(jnp.int32, info_ref.shape, 1).astype(F32)
     member = jnp.where(lane_ids == info_ref[:, 1:2], 1.0, 0.0).astype(BF16)
-    others = sum(dot_f32(member, part) for part in split_bf16(sums, 3))
-    others = others - own_ref[...].astype(F32)
+    own = own_ref[...].astype(F32)
+    others = sum(dot_f32(member, part) for part in split_bf16(by_class[...], 3)) - own
     pos_floor = jnp.maximum(pos_count, 1.0)
     total = jnp.sum(acc_ref[...], axis=1, keepdims=True)
     row_scale = keep * (pos_count / pos_floor) / total
     grad_ref[...] = row_scale * sum_grad_ref[...] - (2.0 * keep / pos_floor) * others
+    same_sum = INV_TEMP * jnp.sum(own * others, axis=1, keepdims=True)
+    loss = keep * (pos_count * jnp.log(total) - same_sum) / pos_floor
+    loss = jnp.sum(loss, axis=0, keepdims=True)
+    loss_ref[...] = jnp.broadcast_to(loss, loss_ref.shape)
 
 
 def keys_kernel(
-    blocks_ref, own_ref, info_ref, scales_ref, same_ref, row_grad_hbm, unit_hbm, length_hbm,
-    picked_hbm, class_hbm, keys_hbm, more_hbm, grad_ref, out_ref,
+    blocks_ref, own_ref, scales_ref, loss_ref, row_grad_hbm, unit_hbm, length_hbm, picked_hbm, class_hbm,
+    keys_hbm, more_hbm, grad_ref, out_ref,
     keys, scale, acc, row_grad, unit, length, picked, sems, end_sems,
 ):
     valid = blocks_before(blocks_ref, blocks_ref.shape[0])
@@ -345,35 +344,35 @@
         copy.start()
     first_place = blocks_before(blocks_ref, lax.axis_index("group"))
     scale[...] = jnp.zeros_like(scale)
-
-    def place_scales(image, block, place):
-        span = pl.ds(pl.multiple_of(place * BLK, BLK), BLK)
-        scale[:, span] = scales_ref[image, block : block + 1, :]
-
-    each_block(blocks_ref, place_scales)
+    place = jnp.int32(0)
+    for image in range(blocks_ref.shape[0]):
+        for block in range(scales_ref.shape[1]):
+            scale[pl.ds(place + block, 1), :] = scales_ref[image, block : block + 1, :]
+        place = place + blocks_ref[image]
     acc[...] = jnp.zeros_like(acc)
     own = own_ref[...]
 
     def visit(tile):
         key_tile = key_tile_of(keys, tile)
-        weights = jnp.exp(dot_f32(own, key_tile, NT) * INV_TEMP) * scale[:, lanes_of(tile)]
+        per_tile = TILE // BLK
+        key_scale = jnp.concatenate(
+            [scale[pl.ds(tile * per_tile + i, 1), :] for i in range(per_tile)], axis=1
+        )
+        weights = jnp.exp(dot_f32(own, key_tile, NT) * INV_TEMP) * key_scale
         weights = jnp.where(not_own(own.shape[0], first_place, tile), weights, 0.0)
         acc[...] += dot_f32(weights.astype(BF16), key_tile)
 
     each_tile(valid, waits, visit)
     for copy in late:
         copy.wait()
-    grad = row_grad[...] + info_ref[:, 0:1] * acc[...]
+    grad = row_grad[...] + acc[...]
     radial = jnp.sum(unit[...] * grad, axis=1, keepdims=True)
-    grad = (grad - unit[...] * radial) / length[:, 0:1]
+    grad = (grad - unit[...] * radial) * length[:, 0:1]
     grad_ref[...] = grad
     width = grad.shape[1]
     out_ref[:, :width] = sum(dot_f32(picked[...], part) for part in split_bf16(grad, 3))
-    scales = scale[...]
-    logs = jnp.where(scales > 0.0, -jnp.log(jnp.where(scales > 0.0, scales, 1.0)), 0.0)
-    loss = jnp.sum(logs, axis=1, keepdims=True) - same_ref[...]
     last = (out_ref.shape[0], 1)
-    out_ref[:, width + BLK - 1 :] = jnp.broadcast_to(loss, last)
+    out_ref[:, width + BLK - 1 :] = jnp.broadcast_to(loss_ref[0:1, 0:1], last)
 
 
 def features_kernel(pix_ref, grad_ref, proj_ref, logits_ref, class_ref, out_ref):
@@ -415,7 +414,7 @@
     proj_ref[...] = summed[:, :width]
     class_ref[...] = summed[:, width : width + classes]
     groups = blocks_ref.shape[0]
-    anchors = (blocks_before(blocks_ref, groups) * (groups * BLK)).astype(F32)
+    anchors = (blocks_before(blocks_ref, groups) * BLK).astype(F32)
     top = summed[:8, width:]
     rows = lax.broadcasted_iota(jnp.int32, top.shape, 0)
     lanes = lax.broadcasted_iota(jnp.int32, top.shape, 1)
@@ -434,7 +433,7 @@
     return jax.ShapeDtypeStruct(shape, dtype)
 
 
-def call(kernel, name, ins, outs, out_specs=None, scratch=(), flops=0, exps=0):
+def call(kernel, name, ins, outs, out_specs=None, scratch=(), flops=0, exps=0, vmem=VMEM_BYTES):
     size = sum(a.size * a.dtype.itemsize for a, _ in ins)
     size += sum(o.size * o.dtype.itemsize for o in outs)
     return pl.pallas_call(
@@ -444,7 +443,7 @@
         in_specs=[s for _, s in ins],
         out_specs=out_specs or [VMEM] * len(outs),
         scratch_shapes=list(scratch),
-        compiler_params=pltpu.CompilerParams(vmem_limit_bytes=VMEM_BYTES),
+        compiler_params=pltpu.CompilerParams(vmem_limit_bytes=vmem),
         cost_estimate=pl.CostEstimate(flops=flops, bytes_accessed=size, transcendentals=exps),
     )(*[a for a, _ in ins])
 
@@ -466,11 +465,10 @@
     share = channels // groups
     valid = jnp.sum(anchor_blocks)
 
-    picked, emb, send = call(
+    emb, send = call(
         pick_kernel, "pick_anchors",
         [(anchor_blocks, SMEM), (anchor_pix, VMEM), (features, ANY), (proj_weight, VMEM)],
-        [shape_of((slots, channels), BF16), shape_of((slots, width), BF16),
-         shape_of((groups, slots // groups, width), BF16)],
+        [shape_of((slots, width), BF16), shape_of((groups, slots // groups, width), BF16)],
         None, [pltpu.VMEM(features.shape, BF16), pltpu.SemaphoreType.DMA((4,))],
         flops=2 * slots * channels * (pixels + width),
     )
@@ -500,12 +498,16 @@
     more = more.reshape(groups, more_units, UNIT, width)
 
     labels, late_features, _ = lax.optimization_barrier((anchor_label, features, rep))
-    key_label, info, lanes, unit, length = call(
+    key_label, info, lanes, unit, scale, picked_t = call(
         label_kernel, "anchor_labels",
-        [(anchor_blocks, SMEM), (labels, VMEM), (picked, VMEM), (proj_weight, VMEM)],
+        [(anchor_blocks, SMEM), (labels, VMEM), (anchor_pix, VMEM), (late_features, ANY),
+         (proj_weight, VMEM)],
         [shape_of((1, blocks * BLK)), shape_of((slots, BLK)), shape_of((8, slots)),
-         shape_of((slots, width)), shape_of((slots, BLK))],
-        None, [pltpu.VMEM((BLK, slots), F32)],
+         shape_of((slots, width)), shape_of((slots, BLK)), shape_of((channels, slots), BF16)],
+        None,
+        [pltpu.VMEM((BLK, slots), F32), pltpu.VMEM(features.shape, BF16),
+         pltpu.SemaphoreType.DMA((4,))],
+        vmem=LABEL_BYTES,
     )
     logits = jnp.dot(late_features, class_weight, preferred_element_type=F32)
     top_logit = jnp.max(logits, axis=1, keepdims=True)
@@ -518,36 +520,34 @@
     tail = jnp.broadcast_to(pixel_loss, (channels, BLK - classes))
     class_part = jnp.concatenate([class_part, tail], axis=1)
     key_scratch = pltpu.VMEM((blocks // 2, 2, PARTS, UNIT, width), BF16)
-    key_sems = [pltpu.SemaphoreType.DMA((3, groups))]
+    key_sems = [pltpu.SemaphoreType.DMA((len(SOON) + 1, groups))]
     pairs = slots * ROOM * BLK
     sum_grad, acc, sums = call(
         sums_kernel, "anchor_sums",
         [(anchor_blocks, SMEM), (lanes, VMEM), (emb, VMEM), (keys, ANY), (more, ANY)],
         [shape_of((slots, width)), shape_of((slots, BLK)), shape_of((groups, per_image, BLK))],
-        None, [key_scratch] + key_sems, flops=4 * pairs * width, exps=pairs,
+        None, [key_scratch] + key_sems, flops=4 * pairs * width, exps=pairs, vmem=MID_BYTES,
     )
     scales = exchange(sums)
-    row_grad, same = call(
+    row_grad, loss = call(
         rows_kernel, "anchor_rows",
         [(anchor_blocks, SMEM), (emb, VMEM), (info, VMEM), (acc, VMEM), (sum_grad, VMEM),
          (key_label, VMEM), (keys, ANY), (more, ANY)],
-        [shape_of((slots, width)), shape_of((1, 1))],
-        None,
-        [key_scratch, pltpu.VMEM((BLK, width), F32), pltpu.VMEM((BLK, width), F32)] + key_sems,
-        flops=6 * ROOM * BLK * BLK * width,
+        [shape_of((slots, width)), shape_of((8, BLK))],
+        None, [key_scratch, pltpu.VMEM((BLK, width), F32)] + key_sems,
+        flops=2 * ROOM * BLK * BLK * width, vmem=MID_BYTES,
     )
     grad_projected, part = call(
         keys_kernel, "anchor_keys",
-        [(anchor_blocks, SMEM), (emb, VMEM), (info, VMEM), (scales, VMEM), (same, VMEM),
-         (row_grad, ANY), (unit, ANY), (length, ANY), (picked.T, ANY), (class_part, ANY),
-         (keys, ANY), (more, ANY)],
+        [(anchor_blocks, SMEM), (emb, VMEM), (scales, VMEM), (loss, VMEM), (row_grad, ANY),
+         (unit, ANY), (scale, ANY), (picked_t, ANY), (class_part, ANY), (keys, ANY), (more, ANY)],
         [shape_of((slots, width)), shape_of((channels, width + BLK))],
         None,
-        [key_scratch, pltpu.VMEM((1, blocks * BLK), F32), pltpu.VMEM((slots, width), F32),
+        [key_scratch, pltpu.VMEM((blocks + 8, BLK), F32), pltpu.VMEM((slots, width), F32),
          pltpu.VMEM((slots, width), F32), pltpu.VMEM((slots, width), F32),
          pltpu.VMEM((slots, BLK), F32), pltpu.VMEM((channels, slots), BF16)]
         + key_sems + [pltpu.SemaphoreType.DMA((5,))],
-        flops=4 * pairs * width, exps=pairs,
+        flops=4 * pairs * width, exps=pairs, vmem=MID_BYTES,
     )
 
     received = exchange(part.reshape(groups, share, width + BLK))
@@ -576,13 +576,14 @@
         functools.partial(add_kernel, classes), "add_shares", [(received, VMEM)],
         [shape_of(received.shape, BF16)], [ANY],
         [pltpu.VMEM(received.shape[1:], BF16), pltpu.SemaphoreType.DMA((groups,))],
+        vmem=SMALL_BYTES,
     )
     summed = exchange(part_rep).reshape(channels, width + BLK)
     grad_proj, grad_class, losses = call(
         functools.partial(end_kernel, float(groups * pixels)), "outputs",
         [(anchor_blocks, SMEM), (summed, VMEM)],
         [shape_of((channels, width)), shape_of((channels, classes)), shape_of((2,))],
-        [VMEM, VMEM, SMEM],
+        [VMEM, VMEM, SMEM], vmem=SMALL_BYTES,
     )
     return (grad_features, grad_proj, grad_class, losses)
 

time: 128 us -> 119 us (0.930)
  Pallas kernels: 43.5 us -> 39.2 us
  other arithmetic: 2.74 us -> 6.38 us
  blocking collectives: 17.6 us -> 15.2 us
  waiting for transfers between devices: 34.1 us -> 32 us
  matrix products: 3.17 us -> 1.57 us
    pallas_call x9, Pallas kernels: 37 us -> 32.7 us  [call(): pl.pallas_call(kernel, name=name, out_shape=outs, in_specs=[s for _, s in...]
    all_to_all x1, blocking collectives: 17.6 us -> 15.2 us  [exchange(): return lax.all_to_all(value, 'group', 0, 0, tiled=True)]
    all_to_all x4, waiting for transfers between devices: 34.1 us -> 32 us  [exchange(): return lax.all_to_all(value, 'group', 0, 0, tiled=True)]
    dot_general x1, matrix products: 2.43 us -> 0.83 us  [per_device(): logits = jnp.dot(late_features, class_weight, preferred_element_type=F32)]
    reduce_sum x1, other arithmetic: 0.16 us -> 1.53 us  [per_device(): jnp.sum(jnp.exp(logits - top_logit), axis=1, keepdims=True)]
  transfers between devices with their start and end apart: 4 -> 4, of which waited for: 4 -> 4; matrix products, arithmetic and copies ran while one was open for 7% -> 8% of each run, Pallas kernels for 13% -> 14%
where the time goes in v2:
time: 119 us
  Pallas kernels  39.2 us (33%)
  waiting for transfers between devices  32 us (27%)
  starting transfers between devices  19.5 us (16%)
  blocking collectives  15.2 us (13%)
  other arithmetic  6.38 us (5%)
  local copies, waits for them, and re-layouts  3.04 us (3%)
  between operations  1.77 us (1%)
  matrix products  1.57 us (1%)
    pallas_call x9, Pallas kernels, call(): pl.pallas_call(kernel, name=name, out_shape=outs, in_specs=[s for _, s in...  32.7 us
    all_to_all x4, waiting for transfers between devices, exchange(): return lax.all_to_all(value, 'group', 0, 0, tiled=True)  32 us
    all_to_all x4, starting transfers between devices, exchange(): return lax.all_to_all(value, 'group', 0, 0, tiled=True)  19.5 us
    all_to_all x1, blocking collectives, exchange(): return lax.all_to_all(value, 'group', 0, 0, tiled=True)  15.2 us
    pallas_call x1, Pallas kernels, per_device(): pl.pallas_call(features_kernel, name='feature_grads', grid=(pixels // til...  6.5 us
    reduce_sum x2, other arithmetic, per_device(): pixel_loss = jnp.sum(logsum_class[:, 0] - jnp.sum(onehot * logits, axis=1))  2.47 us
  transfers between devices with their start and end apart: 4, of which 4 were waited for; matrix products, arithmetic and copies ran while one was open for 8% of the time, Pallas kernels for 14%

profile of v2, /device:TPU:128, one launch (start us, length us, event | category | flops | bytes accessed | tf_op | source)
XLA Modules:
  0.0 118.6 jit_solution(8693924794924248937)
XLA Ops:
  0.6 0.0 copy-start.15
  0.6 5.0 %pick_anchors.1 = (bf16[512,256]{1,0:T(8,128)(2,1)}, bf16[16,32,256]{2,1,0:T(8,128)(2,1)}) custom-call(s32[16]{0:T(128)} %blocks_ref.14, s32[1,512]{1,0:T(1,128)} %pix_ref.5, bf16[2048,512]{1,0:T(8,128)(2,1)} %features_hbm.2, bf16[512,256]{1,0:T(8,128)(2,1)} %proj_ref.5), custom_call_target="tpu_custom_call" | custom-call | flops 1207959552 | bytes 2885696 | tf_op jit(solution)/shard_map/pick_anchors/pallas_call | solution.py:439
  5.7 7.1 %all-to-all-start.1 = ((bf16[16,32,256]{2,1,0:T(8,128)(2,1)}), bf16[16,32,256]{2,1,0:T(8,128)(2,1)S(1)}, u32[]{:S(2)}, u32[]{:S(2)}) async-start(bf16[16,32,256]{2,1,0:T(8,128)(2,1)} %get-tuple-element.36), calls=%async_computation.1 | async-start | bytes 524288 | tf_op jit(solution)/shard_map/all_to_all | solution.py:452
  12.7 0.0 copy-done.15
  12.7 0.6 reduce_sum.36
  14.0 7.2 %all-to-all-done.1.recv_ref = bf16[16,32,256]{2,1,0:T(8,128)(2,1)S(1)} async-done(((bf16[16,32,256]{2,1,0:T(8,128)(2,1)}), bf16[16,32,256]{2,1,0:T(8,128)(2,1)S(1)}, u32[]{:S(2)}, u32[]{:S(2)}) %all-to-all-start.1) | async-done | bytes 262176 | tf_op jit(solution)/shard_map/all_to_all | solution.py:452
  21.2 0.5 conditional.1
  21.2 0.5 skip_keys.1
  21.8 2.7 %pack_keys.3 = bf16[16,320,256]{2,1,0:T(8,128)(2,1)} custom-call(s32[16]{0:T(128)S(1)} %copy-done.15, bf16[16,32,256]{2,1,0:T(8,128)(2,1)S(1)} %all-to-all-done.1.recv_ref), custom_call_target="tpu_custom_call" | custom-call | bytes 2883648 | tf_op jit(solution)/shard_map/pack_keys/pallas_call | solution.py:439
  24.5 0.0 copy-start.8
  24.5 0.0 copy-start.13
  24.5 4.6 %all-to-all-start.2 = ((bf16[16,320,256]{2,1,0:T(8,128)(2,1)}), bf16[16,320,256]{2,1,0:T(8,128)(2,1)}, u32[]{:S(2)}, u32[]{:S(2)}) async-start(bf16[16,320,256]{2,1,0:T(8,128)(2,1)} %pack_keys.3), calls=%async_computation.2 | async-start | bytes 5242880 | tf_op jit(solution)/shard_map/all_to_all | solution.py:452
  29.1 0.8 fusion
  30.0 0.0 copy-start.10
  30.0 1.0 copy-done.10
  30.9 1.3 %copy.11 = f32[2048,124]{1,0:T(8,128)} copy(f32[2048,124]{0,1:T(8,128)S(1)} %get-tuple-element.58) | data formatting | bytes 2031616 | tf_op jit(solution)/shard_map/dot_general | solution.py:512
  32.3 5.4 %anchor_labels.1 = (f32[1,8192]{1,0:T(1,128)}, f32[512,128]{1,0:T(8,128)}, f32[8,512]{1,0:T(8,128)}, f32[512,256]{1,0:T(8,128)}, f32[512,128]{1,0:T(8,128)}, /*index=5*/bf16[512,512]{1,0:T(8,128)(2,1)}) custom-call(s32[16]{0:T(128)S(1)} %copy-done.15, s32[16,512]{1,0:T(8,128)} %labels_ref, s32[1,512]{1,0:T(1,128)} %pix_ref.5, ...), custom_call_target="tpu_custom_call" | custom-call | bytes 4016192 | tf_op jit(solution)/shard_map/anchor_labels/pallas_call | solution.py:439
  37.7 0.0 copy-start.9
  37.7 1.5 %exponential_reduce_fusion = f32[2048]{0:T(1024)S(1)} fusion(f32[2048,124]{0,1:T(8,128)} %copy-done.10, f32[2048]{0:T(1024)S(1)} %get-tuple-element.57), kind=kLoop, calls=%fused_computation.3 | loop fusion | flops 505856 | bytes 1032192 | tf_op jit(solution)/shard_map/reduce_sum | solution.py:514
  39.3 0.0 copy-done.14
  39.3 1.9 %select_reduce_fusion = f32[2048]{0:T(1024)S(1)} fusion(f32[2048,124]{1,0:T(8,128)} %copy.11, s32[2048]{0:T(1024)S(1)} %copy-done.14), kind=kLoop, calls=%fused_computation | loop fusion | flops 759808 | bytes 1032192 | tf_op jit(solution)/shard_map/reduce_sum | solution.py:517
  41.1 0.6 subtract_reduce_fusion
  41.7 1.8 %subtract_convert_fusion.logits_ref = bf16[2048,124]{1,0:T(8,128)(2,1)S(1)} fusion(f32[2048,124]{1,0:T(8,128)} %copy.11, s32[2048]{0:T(1024)S(1)} %copy-done.14, f32[2048]{0:T(1024)S(1)} %get-tuple-element.56), kind=kLoop, calls=%fused_computation.1 | loop fusion | flops 1269760 | bytes 1540096 | tf_op jit(solution)/shard_map/convert_element_type | solution.py:518
  43.5 0.0 copy-done.9
  43.5 0.0 copy-start.12
  43.5 0.0 copy-start
  43.6 0.7 fusion.1
  44.3 0.7 concatenate.3.class_hbm
  45.0 19.0 %all-to-all-done.2 = bf16[16,320,256]{2,1,0:T(8,128)(2,1)} async-done(((bf16[16,320,256]{2,1,0:T(8,128)(2,1)}), bf16[16,320,256]{2,1,0:T(8,128)(2,1)}, u32[]{:S(2)}, u32[]{:S(2)}) %all-to-all-start.2) | async-done | bytes 2621472 | tf_op jit(solution)/shard_map/all_to_all | solution.py:452
  64.0 0.0 copy-done.6
  64.0 0.0 copy-done.11
  64.0 0.0 copy-start.1
  64.0 0.0 copy-start.2
  64.0 6.1 %anchor_sums.1 = (f32[512,256]{1,0:T(8,128)S(1)}, f32[512,128]{1,0:T(8,128)S(1)}, f32[16,4,128]{2,1,0:T(4,128)}) custom-call(s32[16]{0:T(128)S(1)} %copy-done.15, f32[8,512]{1,0:T(8,128)S(1)} %copy-done.6, bf16[512,256]{1,0:T(8,128)(2,1)S(1)} %copy-done, bf16[16,20,16,256]{3,2,1,0:T(8,128)(2,1)} %bitcast.2.keys_hbm, bf16[16,12,16,256]{3,2,1,0:T(8,128)(2,1)S(1)} %copy-done.11), custom_call_target="tpu_custom_call" | custom-call | flops 2684354560 | bytes 5292096 | tf_op jit(solution)/shard_map/anchor_sums/pallas_call | solution.py:439
  70.1 4.2 %all-to-all-start.3 = ((f32[16,4,128]{2,1,0:T(4,128)}), f32[16,4,128]{2,1,0:T(4,128)S(1)}, u32[]{:S(2)}, u32[]{:S(2)}) async-start(f32[16,4,128]{2,1,0:T(4,128)} %get-tuple-element.40), calls=%async_computation.3 | async-start | bytes 65536 | tf_op jit(solution)/shard_map/all_to_all | solution.py:452
  74.3 0.0 copy-start.3
  74.3 0.0 copy-start.4
  74.3 0.0 copy-start.5
  74.4 4.4 %anchor_rows.1 = (f32[512,256]{1,0:T(8,128)S(1)}, f32[8,128]{1,0:T(8,128)S(1)}) custom-call(s32[16]{0:T(128)S(1)} %copy-done.15, bf16[512,256]{1,0:T(8,128)(2,1)S(1)} %copy-done, f32[512,128]{1,0:T(8,128)S(1)} %copy-done.1, f32[512,128]{1,0:T(8,128)S(1)} %get-tuple-element.42.acc_ref, f32[512,256]{1,0:T(8,128)S(1)} %get-tuple-element.43.sum_grad_ref, ...), custom_call_target="tpu_custom_call" | custom-call | flops 335544320 | bytes 6066240 | tf_op jit(solution)/shard_map/anchor_rows/pallas_call | solution.py:439
  78.8 3.1 %all-to-all-done.3.scales_ref = f32[16,4,128]{2,1,0:T(4,128)S(1)} async-done(((f32[16,4,128]{2,1,0:T(4,128)}), f32[16,4,128]{2,1,0:T(4,128)S(1)}, u32[]{:S(2)}, u32[]{:S(2)}) %all-to-all-start.3) | async-done | bytes 32800 | tf_op jit(solution)/shard_map/all_to_all | solution.py:452
  81.9 6.1 %anchor_keys.1 = (f32[512,256]{1,0:T(8,128)S(1)}, f32[512,384]{1,0:T(8,128)S(1)}) custom-call(s32[16]{0:T(128)S(1)} %copy-done.15, bf16[512,256]{1,0:T(8,128)(2,1)S(1)} %copy-done, f32[16,4,128]{2,1,0:T(4,128)S(1)} %all-to-all-done.3.scales_ref, f32[8,128]{1,0:T(8,128)S(1)} %get-tuple-element.45.loss_ref, f32[512,256]{1,0:T(8,128)S(1)} %get-tuple-element.46.row_grad_hbm, ...), custom_call_target="tpu_custom_call" | custom-call | flops 2684354560 | bytes 7901248 | tf_op jit(solution)/shard_map/anchor_keys/pallas_call | solution.py:439
  88.0 0.0 copy-start.7
  88.1 15.2 %all_to_all.30.recv_ref = f32[16,32,384]{2,1,0:T(8,128)S(1)} all-to-all(f32[16,32,384]{2,1,0:T(8,128)S(1)} %bitcast.10), channel_id=1, replica_groups=mesh['dp'=16,'group'=16] {'group'}, dimensions={0} | all-to-all | bytes 1572864 | tf_op jit(solution)/shard_map/all_to_all | solution.py:452
  103.3 0.9 add_shares.1
  104.2 3.6 %all-to-all-start.5 = ((bf16[16,32,384]{2,1,0:T(8,128)(2,1)}), bf16[16,32,384]{2,1,0:T(8,128)(2,1)S(1)}, u32[]{:S(2)}, u32[]{:S(2)}) async-start(bf16[16,32,384]{2,1,0:T(8,128)(2,1)} %add_shares.1), calls=%async_computation.5 | async-start | bytes 786432 | tf_op jit(solution)/shard_map/all_to_all | solution.py:452
  107.9 6.5 %feature_grads.1 = bf16[2048,512]{1,0:T(8,128)(2,1)} custom-call(s32[1,512]{1,0:T(1,128)} %pix_ref.5, f32[512,256]{1,0:T(8,128)} %copy-done.7, bf16[512,256]{1,0:T(8,128)(2,1)} %proj_ref.5, bf16[2048,124]{1,0:T(8,128)(2,1)} %copy-done.12, bf16[512,124]{1,0:T(8,128)(2,1)} %class_ref.1), custom_call_target="tpu_custom_call" | custom-call | flops 2407530496 | bytes 4194304 | tf_op jit(solution)/shard_map/feature_grads/pallas_call | solution.py:555
  114.4 2.6 %all-to-all-done.5 = bf16[16,32,384]{2,1,0:T(8,128)(2,1)S(1)} async-done(((bf16[16,32,384]{2,1,0:T(8,128)(2,1)}), bf16[16,32,384]{2,1,0:T(8,128)(2,1)S(1)}, u32[]{:S(2)}, u32[]{:S(2)}) %all-to-all-start.5) | async-done | bytes 393248 | tf_op jit(solution)/shard_map/all_to_all | solution.py:452
  117.0 1.5 %outputs.1 = (f32[512,256]{1,0:T(8,128)}, f32[512,124]{1,0:T(8,128)}, f32[2]{0:T(128)}) custom-call(s32[16]{0:T(128)S(1)} %copy-done.15, bf16[512,384]{1,0:T(8,128)(2,1)S(1)} %bitcast.9), custom_call_target="tpu_custom_call" | custom-call | bytes 1171528 | tf_op jit(solution)/shard_map/outputs/pallas_call | solution.py:439
  (13 shorter events, 0.0 us)
Async XLA Ops:
  0.6 12.1 %copy-start.15 = (s32[16]{0:T(128)S(1)}, s32[16]{0:T(128)}, u32[]{:S(2)}) copy-start(s32[16]{0:T(128)} %blocks_ref.14) | copy-start | bytes 196
  5.7 15.6 %all-to-all-start.1 = ((bf16[16,32,256]{2,1,0:T(8,128)(2,1)}), bf16[16,32,256]{2,1,0:T(8,128)(2,1)S(1)}, u32[]{:S(2)}, u32[]{:S(2)}) async-start(bf16[16,32,256]{2,1,0:T(8,128)(2,1)} %get-tuple-element.36), calls=%async_computation.1 | async-start | bytes 524288 | tf_op jit(solution)/shard_map/all_to_all | solution.py:452
  24.5 4.6 %copy-start.8 = (bf16[2048,512]{1,0:T(8,128)(2,1)S(1)}, bf16[2048,512]{1,0:T(8,128)(2,1)}, u32[]{:S(2)}) copy-start(bf16[2048,512]{1,0:T(8,128)(2,1)} %features_hbm.2) | copy-start | bytes 6291460
  24.5 4.6 %copy-start.13 = (bf16[512,124]{1,0:T(8,128)(2,1)S(1)}, bf16[512,124]{1,0:T(8,128)(2,1)}, u32[]{:S(2)}) copy-start(bf16[512,124]{1,0:T(8,128)(2,1)} %class_ref.1) | copy-start | bytes 380932
  24.5 39.5 %all-to-all-start.2 = ((bf16[16,320,256]{2,1,0:T(8,128)(2,1)}), bf16[16,320,256]{2,1,0:T(8,128)(2,1)}, u32[]{:S(2)}, u32[]{:S(2)}) async-start(bf16[16,320,256]{2,1,0:T(8,128)(2,1)} %pack_keys.3), calls=%async_computation.2 | async-start | bytes 5242880 | tf_op jit(solution)/shard_map/all_to_all | solution.py:452
  30.0 1.0 copy-start.10
  32.3 7.0 %copy-start.14 = (s32[2048]{0:T(1024)S(1)}, s32[2048]{0:T(1024)}, u32[]{:S(2)}) copy-start(s32[2048]{0:T(1024)} %param.15) | copy-start | bytes 24580
  37.7 5.8 %copy-start.9 = (bf16[2048,512]{1,0:T(8,128)(2,1)S(1)}, bf16[2048,512]{1,0:T(8,128)(2,1)}, u32[]{:S(2)}) copy-start(bf16[2048,512]{1,0:T(8,128)(2,1)} %features_hbm.2) | copy-start | bytes 6291460
  43.5 20.5 %copy-start.12 = (bf16[2048,124]{1,0:T(8,128)(2,1)}, bf16[2048,124]{1,0:T(8,128)(2,1)S(1)}, u32[]{:S(2)}) copy-start(bf16[2048,124]{1,0:T(8,128)(2,1)S(1)} %subtract_convert_fusion.logits_ref) | copy-start | bytes 1523716
  43.5 20.5 %copy-start = (bf16[512,256]{1,0:T(8,128)(2,1)S(1)}, bf16[512,256]{1,0:T(8,128)(2,1)}, u32[]{:S(2)}) copy-start(bf16[512,256]{1,0:T(8,128)(2,1)} %get-tuple-element.35.own_ref) | copy-start | bytes 786436
  43.5 20.5 %copy-start.6 = (f32[8,512]{1,0:T(8,128)S(1)}, f32[8,512]{1,0:T(8,128)}, u32[]{:S(2)}) copy-start(f32[8,512]{1,0:T(8,128)} %get-tuple-element.39.lanes_ref) | copy-start | bytes 49156
  43.5 20.5 %copy-start.11 = (bf16[16,12,16,256]{3,2,1,0:T(8,128)(2,1)S(1)}, bf16[16,12,16,256]{3,2,1,0:T(8,128)(2,1)}, u32[]{:S(2)}) copy-start(bf16[16,12,16,256]{3,2,1,0:T(8,128)(2,1)} %get-tuple-element.59.more_hbm) | copy-start | bytes 4718596
  64.0 10.3 %copy-start.1 = (f32[512,128]{1,0:T(8,128)S(1)}, f32[512,128]{1,0:T(8,128)}, u32[]{:S(2)}) copy-start(f32[512,128]{1,0:T(8,128)} %get-tuple-element.41.info_ref) | copy-start | bytes 786436
  64.0 10.3 %copy-start.2 = (f32[1,8192]{1,0:T(1,128)S(1)}, f32[1,8192]{1,0:T(1,128)}, u32[]{:S(2)}) copy-start(f32[1,8192]{1,0:T(1,128)} %get-tuple-element.44.key_label_ref) | copy-start | bytes 98308
  70.1 11.8 %all-to-all-start.3 = ((f32[16,4,128]{2,1,0:T(4,128)}), f32[16,4,128]{2,1,0:T(4,128)S(1)}, u32[]{:S(2)}, u32[]{:S(2)}) async-start(f32[16,4,128]{2,1,0:T(4,128)} %get-tuple-element.40), calls=%async_computation.3 | async-start | bytes 65536 | tf_op jit(solution)/shard_map/all_to_all | solution.py:452
  74.3 7.6 %copy-start.3 = (f32[512,256]{1,0:T(8,128)S(1)}, f32[512,256]{1,0:T(8,128)}, u32[]{:S(2)}) copy-start(f32[512,256]{1,0:T(8,128)} %get-tuple-element.47.unit_hbm) | copy-start | bytes 1572868
  74.3 7.6 %copy-start.4 = (bf16[512,512]{1,0:T(8,128)(2,1)S(1)}, bf16[512,512]{1,0:T(8,128)(2,1)}, u32[]{:S(2)}) copy-start(bf16[512,512]{1,0:T(8,128)(2,1)} %get-tuple-element.49.picked_hbm) | copy-start | bytes 1572868
  74.3 7.6 %copy-start.5 = (f32[512,128]{1,0:T(8,128)S(1)}, f32[512,128]{1,0:T(8,128)}, u32[]{:S(2)}) copy-start(f32[512,128]{1,0:T(8,128)} %get-tuple-element.48.length_hbm) | copy-start | bytes 786436
  88.0 16.2 %copy-start.7 = (f32[512,256]{1,0:T(8,128)}, f32[512,256]{1,0:T(8,128)S(1)}, u32[]{:S(2)}) copy-start(f32[512,256]{1,0:T(8,128)S(1)} %get-tuple-element.50.grad_ref) | copy-start | bytes 1572868
  104.2 12.8 %all-to-all-start.5 = ((bf16[16,32,384]{2,1,0:T(8,128)(2,1)}), bf16[16,32,384]{2,1,0:T(8,128)(2,1)S(1)}, u32[]{:S(2)}, u32[]{:S(2)}) async-start(bf16[16,32,384]{2,1,0:T(8,128)(2,1)} %add_shares.1), calls=%async_computation.5 | async-start | bytes 786432 | tf_op jit(solution)/shard_map/all_to_all | solution.py:452

commit v3 on v2

--- a/solution.py
+++ b/solution.py
@@ -261,24 +261,22 @@
 
 
 def sums_kernel(
-    blocks_ref, lanes_ref, own_ref, keys_hbm, more_hbm, grad_ref, acc_ref, send_ref,
-    keys, sems,
+    blocks_ref, lanes_ref, own_ref, keys_hbm, more_hbm, acc_ref, send_ref, keys, sems
 ):
     valid = blocks_before(blocks_ref, blocks_ref.shape[0])
     waits = load_keys(valid, keys_hbm, more_hbm, keys, sems)
     first_place = blocks_before(blocks_ref, lax.axis_index("group"))
     acc_ref[...] = jnp.zeros_like(acc_ref)
-    grad_ref[...] = jnp.zeros_like(grad_ref)
     own = own_ref[...]
     lane_ids = lax.broadcasted_iota(jnp.int32, (1, TILE), 1)
 
     def visit(tile):
         key_tile = key_tile_of(keys, tile)
-        in_use = jnp.where(lane_ids < valid * BLK - tile * TILE, 1.0, 0.0)
-        weights = jnp.exp(dot_f32(own, key_tile, NT) * INV_TEMP) * in_use
+        weights = jnp.exp(dot_f32(own, key_tile, NT) * INV_TEMP)
+        if not isinstance(tile, int) or (tile + 1) * TILE > blocks_ref.shape[0] * BLK:
+            weights = weights * jnp.where(lane_ids < valid * BLK - tile * TILE, 1.0, 0.0)
         weights = jnp.where(not_own(own.shape[0], first_place, tile), weights, 0.0)
         acc_ref[...] += fold_lanes(weights)
-        grad_ref[...] += dot_f32(weights.astype(BF16), key_tile)
 
     each_tile(valid, waits, visit)
     for block in range(own.shape[0] // BLK):
@@ -291,8 +289,8 @@
 
 
 def rows_kernel(
-    blocks_ref, own_ref, info_ref, acc_ref, sum_grad_ref, key_label_ref, keys_hbm, more_hbm,
-    grad_ref, loss_ref, keys, by_class, sems,
+    blocks_ref, own_ref, info_ref, acc_ref, key_label_ref, keys_hbm, more_hbm,
+    grad_ref, scale_ref, loss_ref, keys, by_class, sems,
 ):
     valid = blocks_before(blocks_ref, blocks_ref.shape[0])
     waits = load_keys(valid, keys_hbm, more_hbm, keys, sems)
@@ -313,8 +311,8 @@
     others = sum(dot_f32(member, part) for part in split_bf16(by_class[...], 3)) - own
     pos_floor = jnp.maximum(pos_count, 1.0)
     total = jnp.sum(acc_ref[...], axis=1, keepdims=True)
-    row_scale = keep * (pos_count / pos_floor) / total
-    grad_ref[...] = row_scale * sum_grad_ref[...] - (2.0 * keep / pos_floor) * others
+    scale_ref[...] = jnp.broadcast_to((pos_count / pos_floor) / total, scale_ref.shape)
+    grad_ref[...] = (-2.0 * keep / pos_floor) * others
     same_sum = INV_TEMP * jnp.sum(own * others, axis=1, keepdims=True)
     loss = keep * (pos_count * jnp.log(total) - same_sum) / pos_floor
     loss = jnp.sum(loss, axis=0, keepdims=True)
@@ -322,7 +320,7 @@
 
 
 def keys_kernel(
-    blocks_ref, own_ref, scales_ref, loss_ref, row_grad_hbm, unit_hbm, length_hbm, picked_hbm, class_hbm,
+    blocks_ref, own_ref, row_scale_ref, scales_ref, loss_ref, row_grad_hbm, unit_hbm, length_hbm, picked_hbm, class_hbm,
     keys_hbm, more_hbm, grad_ref, out_ref,
     keys, scale, acc, row_grad, unit, length, picked, sems, end_sems,
 ):
@@ -351,6 +349,7 @@
         place = place + blocks_ref[image]
     acc[...] = jnp.zeros_like(acc)
     own = own_ref[...]
+    row_scale = row_scale_ref[:, 0:1]
 
     def visit(tile):
         key_tile = key_tile_of(keys, tile)
@@ -358,7 +357,7 @@
         key_scale = jnp.concatenate(
             [scale[pl.ds(tile * per_tile + i, 1), :] for i in range(per_tile)], axis=1
         )
-        weights = jnp.exp(dot_f32(own, key_tile, NT) * INV_TEMP) * key_scale
+        weights = jnp.exp(dot_f32(own, key_tile, NT) * INV_TEMP) * (row_scale + key_scale)
         weights = jnp.where(not_own(own.shape[0], first_place, tile), weights, 0.0)
         acc[...] += dot_f32(weights.astype(BF16), key_tile)
 
@@ -370,7 +369,7 @@
     grad = (grad - unit[...] * radial) * length[:, 0:1]
     grad_ref[...] = grad
     width = grad.shape[1]
-    out_ref[:, :width] = sum(dot_f32(picked[...], part) for part in split_bf16(grad, 3))
+    out_ref[:, :width] = sum(dot_f32(picked[...], part) for part in split_bf16(grad, 2))
     last = (out_ref.shape[0], 1)
     out_ref[:, width + BLK - 1 :] = jnp.broadcast_to(loss_ref[0:1, 0:1], last)
 
@@ -522,24 +521,24 @@
     key_scratch = pltpu.VMEM((blocks // 2, 2, PARTS, UNIT, width), BF16)
     key_sems = [pltpu.SemaphoreType.DMA((len(SOON) + 1, groups))]
     pairs = slots * ROOM * BLK
-    sum_grad, acc, sums = call(
+    acc, sums = call(
         sums_kernel, "anchor_sums",
         [(anchor_blocks, SMEM), (lanes, VMEM), (emb, VMEM), (keys, ANY), (more, ANY)],
-        [shape_of((slots, width)), shape_of((slots, BLK)), shape_of((groups, per_image, BLK))],
-        None, [key_scratch] + key_sems, flops=4 * pairs * width, exps=pairs, vmem=MID_BYTES,
+        [shape_of((slots, BLK)), shape_of((groups, per_image, BLK))],
+        None, [key_scratch] + key_sems, flops=2 * pairs * width, exps=pairs, vmem=MID_BYTES,
     )
     scales = exchange(sums)
-    row_grad, loss = call(
+    row_grad, row_scale, loss = call(
         rows_kernel, "anchor_rows",
-        [(anchor_blocks, SMEM), (emb, VMEM), (info, VMEM), (acc, VMEM), (sum_grad, VMEM),
-         (key_label, VMEM), (keys, ANY), (more, ANY)],
-        [shape_of((slots, width)), shape_of((8, BLK))],
+        [(anchor_blocks, SMEM), (emb, VMEM), (info, VMEM), (acc, VMEM), (key_label, VMEM),
+         (keys, ANY), (more, ANY)],
+        [shape_of((slots, width)), shape_of((slots, BLK)), shape_of((8, BLK))],
         None, [key_scratch, pltpu.VMEM((BLK, width), F32)] + key_sems,
         flops=2 * ROOM * BLK * BLK * width, vmem=MID_BYTES,
     )
     grad_projected, part = call(
         keys_kernel, "anchor_keys",
-        [(anchor_blocks, SMEM), (emb, VMEM), (scales, VMEM), (loss, VMEM), (row_grad, ANY),
+        [(anchor_blocks, SMEM), (emb, VMEM), (row_scale, VMEM), (scales, VMEM), (loss, VMEM), (row_grad, ANY),
          (unit, ANY), (scale, ANY), (picked_t, ANY), (class_part, ANY), (keys, ANY), (more, ANY)],
         [shape_of((slots, width)), shape_of((channels, width + BLK))],
         None,

time: 119 us -> 119 us (level)
  no operation moved by 1% of the time
where the time goes in v3:
time: 119 us; the launch traced here: 118 us
  Pallas kernels  38.5 us (32%)
  waiting for transfers between devices  32.2 us (27%)
  starting transfers between devices  19.5 us (16%)
  blocking collectives  15 us (13%)
  other arithmetic  6.38 us (5%)
  local copies, waits for them, and re-layouts  3.05 us (3%)
  between operations  1.74 us (1%)
  matrix products  1.59 us (1%)
    all_to_all x4, waiting for transfers between devices, exchange(): return lax.all_to_all(value, 'group', 0, 0, tiled=True)  32.2 us
    pallas_call x9, Pallas kernels, call(): pl.pallas_call(kernel, name=name, out_shape=outs, in_specs=[s for _, s in...  32 us
    all_to_all x4, starting transfers between devices, exchange(): return lax.all_to_all(value, 'group', 0, 0, tiled=True)  19.5 us
    all_to_all x1, blocking collectives, exchange(): return lax.all_to_all(value, 'group', 0, 0, tiled=True)  15 us
    pallas_call x1, Pallas kernels, per_device(): pl.pallas_call(features_kernel, name='feature_grads', grid=(pixels // til...  6.5 us
    reduce_sum x2, other arithmetic, per_device(): pixel_loss = jnp.sum(logsum_class[:, 0] - jnp.sum(onehot * logits, axis=1))  2.47 us
  transfers between devices with their start and end apart: 4, of which 4 were waited for; matrix products, arithmetic and copies ran while one was open for 8% of the time, Pallas kernels for 14%

profile of v3, /device:TPU:128, one launch (start us, length us, event | category | flops | bytes accessed | tf_op | source)
XLA Modules:
  0.0 117.9 jit_solution(109118407767139218)
XLA Ops:
  0.6 0.0 copy-start.14
  0.6 5.0 %pick_anchors.1 = (bf16[512,256]{1,0:T(8,128)(2,1)}, bf16[16,32,256]{2,1,0:T(8,128)(2,1)}) custom-call(s32[16]{0:T(128)} %blocks_ref.14, s32[1,512]{1,0:T(1,128)} %pix_ref.5, bf16[2048,512]{1,0:T(8,128)(2,1)} %features_hbm.2, bf16[512,256]{1,0:T(8,128)(2,1)} %proj_ref.5), custom_call_target="tpu_custom_call" | custom-call | flops 1207959552 | bytes 2885696 | tf_op jit(solution)/shard_map/pick_anchors/pallas_call | solution.py:438
  5.7 7.1 %all-to-all-start.1 = ((bf16[16,32,256]{2,1,0:T(8,128)(2,1)}), bf16[16,32,256]{2,1,0:T(8,128)(2,1)S(1)}, u32[]{:S(2)}, u32[]{:S(2)}) async-start(bf16[16,32,256]{2,1,0:T(8,128)(2,1)} %get-tuple-element.36), calls=%async_computation.1 | async-start | bytes 524288 | tf_op jit(solution)/shard_map/all_to_all | solution.py:451
  12.7 0.0 copy-done.14
  12.7 0.6 reduce_sum.36
  14.0 7.2 %all-to-all-done.1.recv_ref = bf16[16,32,256]{2,1,0:T(8,128)(2,1)S(1)} async-done(((bf16[16,32,256]{2,1,0:T(8,128)(2,1)}), bf16[16,32,256]{2,1,0:T(8,128)(2,1)S(1)}, u32[]{:S(2)}, u32[]{:S(2)}) %all-to-all-start.1) | async-done | bytes 262176 | tf_op jit(solution)/shard_map/all_to_all | solution.py:451
  21.2 0.5 conditional.1
  21.2 0.5 skip_keys.1
  21.8 2.7 %pack_keys.3 = bf16[16,320,256]{2,1,0:T(8,128)(2,1)} custom-call(s32[16]{0:T(128)S(1)} %copy-done.14, bf16[16,32,256]{2,1,0:T(8,128)(2,1)S(1)} %all-to-all-done.1.recv_ref), custom_call_target="tpu_custom_call" | custom-call | bytes 2883648 | tf_op jit(solution)/shard_map/pack_keys/pallas_call | solution.py:438
  24.5 0.0 copy-start.8
  24.5 0.0 copy-start.12
  24.5 4.6 %all-to-all-start.2 = ((bf16[16,320,256]{2,1,0:T(8,128)(2,1)}), bf16[16,320,256]{2,1,0:T(8,128)(2,1)}, u32[]{:S(2)}, u32[]{:S(2)}) async-start(bf16[16,320,256]{2,1,0:T(8,128)(2,1)} %pack_keys.3), calls=%async_computation.2 | async-start | bytes 5242880 | tf_op jit(solution)/shard_map/all_to_all | solution.py:451
  29.1 0.0 copy-done.8
  29.1 0.0 copy-done.12
  29.1 0.8 fusion
  30.0 0.0 copy-start.10
  30.0 1.0 copy-done.10
  31.0 1.3 %copy.11 = f32[2048,124]{1,0:T(8,128)} copy(f32[2048,124]{0,1:T(8,128)S(1)} %get-tuple-element.58) | data formatting | bytes 2031616 | tf_op jit(solution)/shard_map/dot_general | solution.py:511
  32.3 5.4 %anchor_labels.1 = (f32[1,8192]{1,0:T(1,128)}, f32[512,128]{1,0:T(8,128)}, f32[8,512]{1,0:T(8,128)}, f32[512,256]{1,0:T(8,128)}, f32[512,128]{1,0:T(8,128)}, /*index=5*/bf16[512,512]{1,0:T(8,128)(2,1)}) custom-call(s32[16]{0:T(128)S(1)} %copy-done.14, s32[16,512]{1,0:T(8,128)} %labels_ref, s32[1,512]{1,0:T(1,128)} %pix_ref.5, ...), custom_call_target="tpu_custom_call" | custom-call | bytes 4016192 | tf_op jit(solution)/shard_map/anchor_labels/pallas_call | solution.py:438
  37.8 0.0 copy-start.9
  37.8 1.5 %exponential_reduce_fusion = f32[2048]{0:T(1024)S(1)} fusion(f32[2048,124]{0,1:T(8,128)} %copy-done.10, f32[2048]{0:T(1024)S(1)} %get-tuple-element.57), kind=kLoop, calls=%fused_computation.3 | loop fusion | flops 505856 | bytes 1032192 | tf_op jit(solution)/shard_map/reduce_sum | solution.py:513
  39.3 0.0 copy-done.13
  39.3 1.9 %select_reduce_fusion = f32[2048]{0:T(1024)S(1)} fusion(f32[2048,124]{1,0:T(8,128)} %copy.11, s32[2048]{0:T(1024)S(1)} %copy-done.13), kind=kLoop, calls=%fused_computation | loop fusion | flops 759808 | bytes 1032192 | tf_op jit(solution)/shard_map/reduce_sum | solution.py:516
  41.2 0.6 subtract_reduce_fusion
  41.8 1.8 %subtract_convert_fusion.logits_ref = bf16[2048,124]{1,0:T(8,128)(2,1)S(1)} fusion(f32[2048,124]{1,0:T(8,128)} %copy.11, s32[2048]{0:T(1024)S(1)} %copy-done.13, f32[2048]{0:T(1024)S(1)} %get-tuple-element.56), kind=kLoop, calls=%fused_computation.1 | loop fusion | flops 1269760 | bytes 1540096 | tf_op jit(solution)/shard_map/convert_element_type | solution.py:517
  43.5 0.0 copy-done.9
  43.5 0.0 copy-start.11
  43.6 0.0 copy-start
  43.6 0.0 copy-start.6
  43.6 0.7 fusion.1
  44.3 0.0 copy-done.11
  44.3 0.7 concatenate.3.class_hbm
  45.0 19.0 %all-to-all-done.2 = bf16[16,320,256]{2,1,0:T(8,128)(2,1)} async-done(((bf16[16,320,256]{2,1,0:T(8,128)(2,1)}), bf16[16,320,256]{2,1,0:T(8,128)(2,1)}, u32[]{:S(2)}, u32[]{:S(2)}) %all-to-all-start.2) | async-done | bytes 2621472 | tf_op jit(solution)/shard_map/all_to_all | solution.py:451
  64.0 0.0 copy-done
  64.0 5.8 %anchor_sums.1 = (f32[512,128]{1,0:T(8,128)S(1)}, f32[16,4,128]{2,1,0:T(4,128)}) custom-call(s32[16]{0:T(128)S(1)} %copy-done.14, f32[8,512]{1,0:T(8,128)S(1)} %copy-done.6, bf16[512,256]{1,0:T(8,128)(2,1)S(1)} %copy-done, bf16[16,20,16,256]{3,2,1,0:T(8,128)(2,1)} %bitcast.2.keys_hbm, bf16[16,12,16,256]{3,2,1,0:T(8,128)(2,1)} %get-tuple-element.59.more_hbm), custom_call_target="tpu_custom_call" | custom-call | flops 1342177280 | bytes 4767808 | tf_op jit(solution)/shard_map/anchor_sums/pallas_call | solution.py:438
  69.8 4.2 %all-to-all-start.3 = ((f32[16,4,128]{2,1,0:T(4,128)}), f32[16,4,128]{2,1,0:T(4,128)S(1)}, u32[]{:S(2)}, u32[]{:S(2)}) async-start(f32[16,4,128]{2,1,0:T(4,128)} %get-tuple-element.44), calls=%async_computation.3 | async-start | bytes 65536 | tf_op jit(solution)/shard_map/all_to_all | solution.py:451
  74.0 0.0 copy-start.3
  74.1 4.2 %anchor_rows.1 = (f32[512,256]{1,0:T(8,128)S(1)}, f32[512,128]{1,0:T(8,128)S(1)}, f32[8,128]{1,0:T(8,128)S(1)}) custom-call(s32[16]{0:T(128)S(1)} %copy-done.14, bf16[512,256]{1,0:T(8,128)(2,1)S(1)} %copy-done, f32[512,128]{1,0:T(8,128)S(1)} %copy-done.1, f32[512,128]{1,0:T(8,128)S(1)} %get-tuple-element.41.acc_ref, f32[1,8192]{1,0:T(1,128)S(1)} %copy-done.2, ...), custom_call_target="tpu_custom_call" | custom-call | flops 335544320 | bytes 5804096 | tf_op jit(solution)/shard_map/anchor_rows/pallas_call | solution.py:438
  78.3 3.4 %all-to-all-done.3.scales_ref = f32[16,4,128]{2,1,0:T(4,128)S(1)} async-done(((f32[16,4,128]{2,1,0:T(4,128)}), f32[16,4,128]{2,1,0:T(4,128)S(1)}, u32[]{:S(2)}, u32[]{:S(2)}) %all-to-all-start.3) | async-done | bytes 32800 | tf_op jit(solution)/shard_map/all_to_all | solution.py:451
  81.6 0.0 copy-done.5
  81.6 5.9 %anchor_keys.1 = (f32[512,256]{1,0:T(8,128)S(1)}, f32[512,384]{1,0:T(8,128)S(1)}) custom-call(s32[16]{0:T(128)S(1)} %copy-done.14, bf16[512,256]{1,0:T(8,128)(2,1)S(1)} %copy-done, f32[512,128]{1,0:T(8,128)S(1)} %get-tuple-element.43.row_scale_ref, f32[16,4,128]{2,1,0:T(4,128)S(1)} %all-to-all-done.3.scales_ref, f32[8,128]{1,0:T(8,128)S(1)} %get-tuple-element.45.loss_ref, ...), custom_call_target="tpu_custom_call" | custom-call | flops 2684354560 | bytes 8163392 | tf_op jit(solution)/shard_map/anchor_keys/pallas_call | solution.py:438
  87.6 0.0 copy-start.7
  87.6 15.0 %all_to_all.30.recv_ref = f32[16,32,384]{2,1,0:T(8,128)S(1)} all-to-all(f32[16,32,384]{2,1,0:T(8,128)S(1)} %bitcast.10), channel_id=1, replica_groups=mesh['dp'=16,'group'=16] {'group'}, dimensions={0} | all-to-all | bytes 1572864 | tf_op jit(solution)/shard_map/all_to_all | solution.py:451
  102.6 0.9 add_shares.1
  103.5 3.6 %all-to-all-start.5 = ((bf16[16,32,384]{2,1,0:T(8,128)(2,1)}), bf16[16,32,384]{2,1,0:T(8,128)(2,1)S(1)}, u32[]{:S(2)}, u32[]{:S(2)}) async-start(bf16[16,32,384]{2,1,0:T(8,128)(2,1)} %add_shares.1), calls=%async_computation.5 | async-start | bytes 786432 | tf_op jit(solution)/shard_map/all_to_all | solution.py:451
  107.2 6.5 %feature_grads.1 = bf16[2048,512]{1,0:T(8,128)(2,1)} custom-call(s32[1,512]{1,0:T(1,128)} %pix_ref.5, f32[512,256]{1,0:T(8,128)} %copy-done.7, bf16[512,256]{1,0:T(8,128)(2,1)} %proj_ref.5, bf16[2048,124]{1,0:T(8,128)(2,1)} %copy-done.11, bf16[512,124]{1,0:T(8,128)(2,1)} %class_ref.1), custom_call_target="tpu_custom_call" | custom-call | flops 2407530496 | bytes 4194304 | tf_op jit(solution)/shard_map/feature_grads/pallas_call | solution.py:554
  113.7 2.6 %all-to-all-done.5 = bf16[16,32,384]{2,1,0:T(8,128)(2,1)S(1)} async-done(((bf16[16,32,384]{2,1,0:T(8,128)(2,1)}), bf16[16,32,384]{2,1,0:T(8,128)(2,1)S(1)}, u32[]{:S(2)}, u32[]{:S(2)}) %all-to-all-start.5) | async-done | bytes 393248 | tf_op jit(solution)/shard_map/all_to_all | solution.py:451
  116.3 1.5 %outputs.1 = (f32[512,256]{1,0:T(8,128)}, f32[512,124]{1,0:T(8,128)}, f32[2]{0:T(128)}) custom-call(s32[16]{0:T(128)S(1)} %copy-done.14, bf16[512,384]{1,0:T(8,128)(2,1)S(1)} %bitcast.9), custom_call_target="tpu_custom_call" | custom-call | bytes 1171528 | tf_op jit(solution)/shard_map/outputs/pallas_call | solution.py:438
  (11 shorter events, 0.0 us)
Async XLA Ops:
  0.6 12.1 %copy-start.14 = (s32[16]{0:T(128)S(1)}, s32[16]{0:T(128)}, u32[]{:S(2)}) copy-start(s32[16]{0:T(128)} %blocks_ref.14) | copy-start | bytes 196
  5.7 15.6 %all-to-all-start.1 = ((bf16[16,32,256]{2,1,0:T(8,128)(2,1)}), bf16[16,32,256]{2,1,0:T(8,128)(2,1)S(1)}, u32[]{:S(2)}, u32[]{:S(2)}) async-start(bf16[16,32,256]{2,1,0:T(8,128)(2,1)} %get-tuple-element.36), calls=%async_computation.1 | async-start | bytes 524288 | tf_op jit(solution)/shard_map/all_to_all | solution.py:451
  24.5 4.6 %copy-start.8 = (bf16[2048,512]{1,0:T(8,128)(2,1)S(1)}, bf16[2048,512]{1,0:T(8,128)(2,1)}, u32[]{:S(2)}) copy-start(bf16[2048,512]{1,0:T(8,128)(2,1)} %features_hbm.2) | copy-start | bytes 6291460
  24.5 4.6 %copy-start.12 = (bf16[512,124]{1,0:T(8,128)(2,1)S(1)}, bf16[512,124]{1,0:T(8,128)(2,1)}, u32[]{:S(2)}) copy-start(bf16[512,124]{1,0:T(8,128)(2,1)} %class_ref.1) | copy-start | bytes 380932
  24.5 39.5 %all-to-all-start.2 = ((bf16[16,320,256]{2,1,0:T(8,128)(2,1)}), bf16[16,320,256]{2,1,0:T(8,128)(2,1)}, u32[]{:S(2)}, u32[]{:S(2)}) async-start(bf16[16,320,256]{2,1,0:T(8,128)(2,1)} %pack_keys.3), calls=%async_computation.2 | async-start | bytes 5242880 | tf_op jit(solution)/shard_map/all_to_all | solution.py:451
  30.0 1.0 copy-start.10
  32.3 7.0 %copy-start.13 = (s32[2048]{0:T(1024)S(1)}, s32[2048]{0:T(1024)}, u32[]{:S(2)}) copy-start(s32[2048]{0:T(1024)} %param.15) | copy-start | bytes 24580
  37.8 5.8 %copy-start.9 = (bf16[2048,512]{1,0:T(8,128)(2,1)S(1)}, bf16[2048,512]{1,0:T(8,128)(2,1)}, u32[]{:S(2)}) copy-start(bf16[2048,512]{1,0:T(8,128)(2,1)} %features_hbm.2) | copy-start | bytes 6291460
  43.5 0.8 copy-start.11
  43.6 20.4 %copy-start = (bf16[512,256]{1,0:T(8,128)(2,1)S(1)}, bf16[512,256]{1,0:T(8,128)(2,1)}, u32[]{:S(2)}) copy-start(bf16[512,256]{1,0:T(8,128)(2,1)} %get-tuple-element.35.own_ref) | copy-start | bytes 786436
  43.6 20.4 %copy-start.6 = (f32[8,512]{1,0:T(8,128)S(1)}, f32[8,512]{1,0:T(8,128)}, u32[]{:S(2)}) copy-start(f32[8,512]{1,0:T(8,128)} %get-tuple-element.40.lanes_ref) | copy-start | bytes 49156
  64.0 10.0 %copy-start.1 = (f32[512,128]{1,0:T(8,128)S(1)}, f32[512,128]{1,0:T(8,128)}, u32[]{:S(2)}) copy-start(f32[512,128]{1,0:T(8,128)} %get-tuple-element.39.info_ref) | copy-start | bytes 786436
  64.0 10.0 %copy-start.2 = (f32[1,8192]{1,0:T(1,128)S(1)}, f32[1,8192]{1,0:T(1,128)}, u32[]{:S(2)}) copy-start(f32[1,8192]{1,0:T(1,128)} %get-tuple-element.42.key_label_ref) | copy-start | bytes 98308
  69.8 11.8 %all-to-all-start.3 = ((f32[16,4,128]{2,1,0:T(4,128)}), f32[16,4,128]{2,1,0:T(4,128)S(1)}, u32[]{:S(2)}, u32[]{:S(2)}) async-start(f32[16,4,128]{2,1,0:T(4,128)} %get-tuple-element.44), calls=%async_computation.3 | async-start | bytes 65536 | tf_op jit(solution)/shard_map/all_to_all | solution.py:451
  74.0 7.6 %copy-start.3 = (f32[512,256]{1,0:T(8,128)S(1)}, f32[512,256]{1,0:T(8,128)}, u32[]{:S(2)}) copy-start(f32[512,256]{1,0:T(8,128)} %get-tuple-element.47.unit_hbm) | copy-start | bytes 1572868
  74.0 7.6 %copy-start.4 = (bf16[512,512]{1,0:T(8,128)(2,1)S(1)}, bf16[512,512]{1,0:T(8,128)(2,1)}, u32[]{:S(2)}) copy-start(bf16[512,512]{1,0:T(8,128)(2,1)} %get-tuple-element.49.picked_hbm) | copy-start | bytes 1572868
  74.0 7.6 %copy-start.5 = (f32[512,128]{1,0:T(8,128)S(1)}, f32[512,128]{1,0:T(8,128)}, u32[]{:S(2)}) copy-start(f32[512,128]{1,0:T(8,128)} %get-tuple-element.48.length_hbm) | copy-start | bytes 786436
  87.6 16.0 %copy-start.7 = (f32[512,256]{1,0:T(8,128)}, f32[512,256]{1,0:T(8,128)S(1)}, u32[]{:S(2)}) copy-start(f32[512,256]{1,0:T(8,128)S(1)} %get-tuple-element.50.grad_ref) | copy-start | bytes 1572868
  103.5 12.8 %all-to-all-start.5 = ((bf16[16,32,384]{2,1,0:T(8,128)(2,1)}), bf16[16,32,384]{2,1,0:T(8,128)(2,1)S(1)}, u32[]{:S(2)}, u32[]{:S(2)}) async-start(bf16[16,32,384]{2,1,0:T(8,128)(2,1)} %add_shares.1), calls=%async_computation.5 | async-start | bytes 786432 | tf_op jit(solution)/shard_map/all_to_all | solution.py:451

commit v4 on v3

--- a/solution.py
+++ b/solution.py
@@ -8,11 +8,12 @@
 from jax.sharding import PartitionSpec as P
 
 BLK = 128
-SOON = (0, 2, 8)
+SOON = (0, 4, 12)
 UNIT = 16
 PARTS = BLK // UNIT
-TILE = 512
+TILE = 1024
 ROOM = 40
+PAIRS = TILE // (2 * BLK)
 INV_TEMP = 10.0
 EXP_SCALE = INV_TEMP * 1.4426950408889634
 NORM_EPS = 1e-06
@@ -69,8 +70,8 @@
 
 def project(picked, proj):
     projected = dot_f32(picked, proj)
-    length = jnp.sqrt(jnp.sum(projected * projected, axis=1, keepdims=True) + NORM_EPS)
-    return projected / length, length
+    inverse = lax.rsqrt(jnp.sum(projected * projected, axis=1, keepdims=True) + NORM_EPS)
+    return projected * inverse, inverse
 
 
 def pick(pix_ref, features_hbm, features, sems, beside):
@@ -124,9 +125,9 @@
 
     picked = pick(pix_ref, features_hbm, features, sems, labels)
     picked_ref[...] = picked.T.astype(BF16)
-    unit, length = project(picked.astype(BF16), proj_ref[...])
+    unit, inverse = project(picked.astype(BF16), proj_ref[...])
     unit_ref[...] = unit
-    scale_ref[...] = jnp.broadcast_to(info_ref[:, 0:1] / length, scale_ref.shape)
+    scale_ref[...] = jnp.broadcast_to(info_ref[:, 0:1] * inverse, scale_ref.shape)
 
 
 def label_terms(blocks_ref, labels_ref, key_label_ref, info_ref, lanes_ref, wide):
@@ -161,26 +162,23 @@
 
 
 def pack_kernel(first_unit, blocks_ref, recv_ref, rep_hbm, packed, sems):
-    half = lax.div(lax.axis_index("group"), PARTS)
+    half = lax.axis_index("group") >> (PARTS.bit_length() - 1)
     packed[...] = jnp.zeros_like(packed)
     units = packed.shape[0] // UNIT
-
-    def one_image(image, place):
-        odd = lax.rem(place, 2)
-        first = half + odd - 2 * half * odd
+    place = jnp.int32(0)
+    for image in range(blocks_ref.shape[0]):
+        first = half ^ (place & 1)
         for pair in range(2):
             block = 2 * pair + first
-            unit = lax.div(place + block, 2) - first_unit
-
-            @pl.when((block < blocks_ref[image]) & (unit >= 0) & (unit < units))
-            def _():
+            unit = ((place + block) >> 1) - first_unit
+
+            def move(unit=unit, image=image, pair=pair):
                 packed[pl.ds(pl.multiple_of(unit * UNIT, UNIT), UNIT), :] = recv_ref[
                     image, pair * UNIT : (pair + 1) * UNIT, :
                 ]
 
-        return place + blocks_ref[image]
-
-    lax.fori_loop(0, blocks_ref.shape[0], one_image, jnp.int32(0))
+            pl.when((block < blocks_ref[image]) & (unit >= 0) & (unit < units))(move)
+        place = place + blocks_ref[image]
     copies = [
         pltpu.make_async_copy(packed, rep_hbm.at[device], sems.at[device])
         for device in range(rep_hbm.shape[0])
@@ -215,7 +213,7 @@
         copies = copies_of(which, keys_hbm, start, end - start, start)
         for copy in copies:
             copy.start()
-        waits[start // 2] = copies
+        waits[start // PAIRS] = copies
     last = copies_of(len(SOON), more_hbm, 0, more, units)
 
     @pl.when(valid > ROOM)
@@ -246,7 +244,7 @@
 
 
 def key_tile_of(keys, tile):
-    return keys[pl.ds(2 * tile, 2)].reshape(TILE, keys.shape[-1])
+    return keys[pl.ds(PAIRS * tile, PAIRS)].reshape(TILE, keys.shape[-1])
 
 
 def lanes_of(tile):

time: 119 us -> 120 us (level)
  Pallas kernels: 38.5 us -> 39.9 us
    pallas_call x9, Pallas kernels: 32 us -> 33.4 us  [call(): pl.pallas_call(kernel, name=name, out_shape=outs, in_specs=[s for _, s in...]
where the time goes in v4:
time: 120 us; the launch traced here: 119 us
  Pallas kernels  39.9 us (33%)
  waiting for transfers between devices  32 us (27%)
  starting transfers between devices  19.5 us (16%)
  blocking collectives  15 us (12%)
  other arithmetic  6.38 us (5%)
  local copies, waits for them, and re-layouts  3.05 us (3%)
  between operations  1.74 us (1%)
  matrix products  1.59 us (1%)
    pallas_call x9, Pallas kernels, call(): pl.pallas_call(kernel, name=name, out_shape=outs, in_specs=[s for _, s in...  33.4 us
    all_to_all x4, waiting for transfers between devices, exchange(): return lax.all_to_all(value, 'group', 0, 0, tiled=True)  32 us
    all_to_all x4, starting transfers between devices, exchange(): return lax.all_to_all(value, 'group', 0, 0, tiled=True)  19.5 us
    all_to_all x1, blocking collectives, exchange(): return lax.all_to_all(value, 'group', 0, 0, tiled=True)  15 us
    pallas_call x1, Pallas kernels, per_device(): pl.pallas_call(features_kernel, name='feature_grads', grid=(pixels // til...  6.5 us
    reduce_sum x2, other arithmetic, per_device(): pixel_loss = jnp.sum(logsum_class[:, 0] - jnp.sum(onehot * logits, axis=1))  2.47 us
  transfers between devices with their start and end apart: 4, of which 4 were waited for; matrix products, arithmetic and copies ran while one was open for 8% of the time, Pallas kernels for 14%

profile of v4, /device:TPU:128, one launch (start us, length us, event | category | flops | bytes accessed | tf_op | source)
XLA Modules:
  0.0 119.1 jit_solution(12330696712157977408)
XLA Ops:
  0.6 0.0 copy-start.14
  0.6 5.0 %pick_anchors.1 = (bf16[512,256]{1,0:T(8,128)(2,1)}, bf16[16,32,256]{2,1,0:T(8,128)(2,1)}) custom-call(s32[16]{0:T(128)} %blocks_ref.14, s32[1,512]{1,0:T(1,128)} %pix_ref.5, bf16[2048,512]{1,0:T(8,128)(2,1)} %features_hbm.2, bf16[512,256]{1,0:T(8,128)(2,1)} %proj_ref.5), custom_call_target="tpu_custom_call" | custom-call | flops 1207959552 | bytes 2885696 | tf_op jit(solution)/shard_map/pick_anchors/pallas_call | solution.py:436
  5.6 7.1 %all-to-all-start.1 = ((bf16[16,32,256]{2,1,0:T(8,128)(2,1)}), bf16[16,32,256]{2,1,0:T(8,128)(2,1)S(1)}, u32[]{:S(2)}, u32[]{:S(2)}) async-start(bf16[16,32,256]{2,1,0:T(8,128)(2,1)} %get-tuple-element.36), calls=%async_computation.1 | async-start | bytes 524288 | tf_op jit(solution)/shard_map/all_to_all | solution.py:449
  12.7 0.0 copy-done.14
  12.7 0.6 reduce_sum.36
  14.0 7.2 %all-to-all-done.1.recv_ref = bf16[16,32,256]{2,1,0:T(8,128)(2,1)S(1)} async-done(((bf16[16,32,256]{2,1,0:T(8,128)(2,1)}), bf16[16,32,256]{2,1,0:T(8,128)(2,1)S(1)}, u32[]{:S(2)}, u32[]{:S(2)}) %all-to-all-start.1) | async-done | bytes 262176 | tf_op jit(solution)/shard_map/all_to_all | solution.py:449
  21.2 0.5 conditional.1
  21.2 0.5 skip_keys.1
  21.8 2.5 %pack_keys.3 = bf16[16,320,256]{2,1,0:T(8,128)(2,1)} custom-call(s32[16]{0:T(128)S(1)} %copy-done.14, bf16[16,32,256]{2,1,0:T(8,128)(2,1)S(1)} %all-to-all-done.1.recv_ref), custom_call_target="tpu_custom_call" | custom-call | bytes 2883648 | tf_op jit(solution)/shard_map/pack_keys/pallas_call | solution.py:436
  24.3 0.0 copy-start.8
  24.3 0.0 copy-start.12
  24.3 4.6 %all-to-all-start.2 = ((bf16[16,320,256]{2,1,0:T(8,128)(2,1)}), bf16[16,320,256]{2,1,0:T(8,128)(2,1)}, u32[]{:S(2)}, u32[]{:S(2)}) async-start(bf16[16,320,256]{2,1,0:T(8,128)(2,1)} %pack_keys.3), calls=%async_computation.2 | async-start | bytes 5242880 | tf_op jit(solution)/shard_map/all_to_all | solution.py:449
  28.9 0.0 copy-done.8
  29.0 0.0 copy-done.12
  29.0 0.8 fusion
  29.8 0.0 copy-start.10
  29.8 1.0 copy-done.10
  30.8 1.3 %copy.11 = f32[2048,124]{1,0:T(8,128)} copy(f32[2048,124]{0,1:T(8,128)S(1)} %get-tuple-element.58) | data formatting | bytes 2031616 | tf_op jit(solution)/shard_map/dot_general | solution.py:509
  32.1 5.6 %anchor_labels.1 = (f32[1,8192]{1,0:T(1,128)}, f32[512,128]{1,0:T(8,128)}, f32[8,512]{1,0:T(8,128)}, f32[512,256]{1,0:T(8,128)}, f32[512,128]{1,0:T(8,128)}, /*index=5*/bf16[512,512]{1,0:T(8,128)(2,1)}) custom-call(s32[16]{0:T(128)S(1)} %copy-done.14, s32[16,512]{1,0:T(8,128)} %labels_ref, s32[1,512]{1,0:T(1,128)} %pix_ref.5, ...), custom_call_target="tpu_custom_call" | custom-call | bytes 4016192 | tf_op jit(solution)/shard_map/anchor_labels/pallas_call | solution.py:436
  37.8 0.0 copy-start.9
  37.8 1.5 %exponential_reduce_fusion = f32[2048]{0:T(1024)S(1)} fusion(f32[2048,124]{0,1:T(8,128)} %copy-done.10, f32[2048]{0:T(1024)S(1)} %get-tuple-element.57), kind=kLoop, calls=%fused_computation.3 | loop fusion | flops 505856 | bytes 1032192 | tf_op jit(solution)/shard_map/reduce_sum | solution.py:511
  39.3 0.0 copy-done.13
  39.3 1.9 %select_reduce_fusion = f32[2048]{0:T(1024)S(1)} fusion(f32[2048,124]{1,0:T(8,128)} %copy.11, s32[2048]{0:T(1024)S(1)} %copy-done.13), kind=kLoop, calls=%fused_computation | loop fusion | flops 759808 | bytes 1032192 | tf_op jit(solution)/shard_map/reduce_sum | solution.py:514
  41.2 0.6 subtract_reduce_fusion
  41.8 1.8 %subtract_convert_fusion.logits_ref = bf16[2048,124]{1,0:T(8,128)(2,1)S(1)} fusion(f32[2048,124]{1,0:T(8,128)} %copy.11, s32[2048]{0:T(1024)S(1)} %copy-done.13, f32[2048]{0:T(1024)S(1)} %get-tuple-element.56), kind=kLoop, calls=%fused_computation.1 | loop fusion | flops 1269760 | bytes 1540096 | tf_op jit(solution)/shard_map/convert_element_type | solution.py:515
  43.6 0.0 copy-done.9
  43.6 0.0 copy-start.11
  43.6 0.0 copy-start
  43.6 0.7 fusion.1
  44.4 0.0 copy-done.11
  44.4 0.7 concatenate.3.class_hbm
  45.0 18.8 %all-to-all-done.2 = bf16[16,320,256]{2,1,0:T(8,128)(2,1)} async-done(((bf16[16,320,256]{2,1,0:T(8,128)(2,1)}), bf16[16,320,256]{2,1,0:T(8,128)(2,1)}, u32[]{:S(2)}, u32[]{:S(2)}) %all-to-all-start.2) | async-done | bytes 2621472 | tf_op jit(solution)/shard_map/all_to_all | solution.py:449
  63.8 0.0 copy-done.6
  63.9 6.4 %anchor_sums.1 = (f32[512,128]{1,0:T(8,128)S(1)}, f32[16,4,128]{2,1,0:T(4,128)}) custom-call(s32[16]{0:T(128)S(1)} %copy-done.14, f32[8,512]{1,0:T(8,128)S(1)} %copy-done.6, bf16[512,256]{1,0:T(8,128)(2,1)S(1)} %copy-done, bf16[16,20,16,256]{3,2,1,0:T(8,128)(2,1)} %bitcast.2.keys_hbm, bf16[16,12,16,256]{3,2,1,0:T(8,128)(2,1)} %get-tuple-element.59.more_hbm), custom_call_target="tpu_custom_call" | custom-call | flops 1342177280 | bytes 4767808 | tf_op jit(solution)/shard_map/anchor_sums/pallas_call | solution.py:436
  70.3 4.2 %all-to-all-start.3 = ((f32[16,4,128]{2,1,0:T(4,128)}), f32[16,4,128]{2,1,0:T(4,128)S(1)}, u32[]{:S(2)}, u32[]{:S(2)}) async-start(f32[16,4,128]{2,1,0:T(4,128)} %get-tuple-element.44), calls=%async_computation.3 | async-start | bytes 65536 | tf_op jit(solution)/shard_map/all_to_all | solution.py:449
  74.5 0.0 copy-start.3
  74.5 0.0 copy-start.4
  74.5 0.0 copy-start.5
  74.5 4.2 %anchor_rows.1 = (f32[512,256]{1,0:T(8,128)S(1)}, f32[512,128]{1,0:T(8,128)S(1)}, f32[8,128]{1,0:T(8,128)S(1)}) custom-call(s32[16]{0:T(128)S(1)} %copy-done.14, bf16[512,256]{1,0:T(8,128)(2,1)S(1)} %copy-done, f32[512,128]{1,0:T(8,128)S(1)} %copy-done.1, f32[512,128]{1,0:T(8,128)S(1)} %get-tuple-element.41.acc_ref, f32[1,8192]{1,0:T(1,128)S(1)} %copy-done.2, ...), custom_call_target="tpu_custom_call" | custom-call | flops 335544320 | bytes 5804096 | tf_op jit(solution)/shard_map/anchor_rows/pallas_call | solution.py:436
  78.7 3.4 %all-to-all-done.3.scales_ref = f32[16,4,128]{2,1,0:T(4,128)S(1)} async-done(((f32[16,4,128]{2,1,0:T(4,128)}), f32[16,4,128]{2,1,0:T(4,128)S(1)}, u32[]{:S(2)}, u32[]{:S(2)}) %all-to-all-start.3) | async-done | bytes 32800 | tf_op jit(solution)/shard_map/all_to_all | solution.py:449
  82.1 6.7 %anchor_keys.1 = (f32[512,256]{1,0:T(8,128)S(1)}, f32[512,384]{1,0:T(8,128)S(1)}) custom-call(s32[16]{0:T(128)S(1)} %copy-done.14, bf16[512,256]{1,0:T(8,128)(2,1)S(1)} %copy-done, f32[512,128]{1,0:T(8,128)S(1)} %get-tuple-element.43.row_scale_ref, f32[16,4,128]{2,1,0:T(4,128)S(1)} %all-to-all-done.3.scales_ref, f32[8,128]{1,0:T(8,128)S(1)} %get-tuple-element.45.loss_ref, ...), custom_call_target="tpu_custom_call" | custom-call | flops 2684354560 | bytes 8163392 | tf_op jit(solution)/shard_map/anchor_keys/pallas_call | solution.py:436
  88.8 0.0 copy-start.7
  88.8 15.0 %all_to_all.30.recv_ref = f32[16,32,384]{2,1,0:T(8,128)S(1)} all-to-all(f32[16,32,384]{2,1,0:T(8,128)S(1)} %bitcast.10), channel_id=1, replica_groups=mesh['dp'=16,'group'=16] {'group'}, dimensions={0} | all-to-all | bytes 1572864 | tf_op jit(solution)/shard_map/all_to_all | solution.py:449
  103.8 0.9 add_shares.1
  104.7 3.6 %all-to-all-start.5 = ((bf16[16,32,384]{2,1,0:T(8,128)(2,1)}), bf16[16,32,384]{2,1,0:T(8,128)(2,1)S(1)}, u32[]{:S(2)}, u32[]{:S(2)}) async-start(bf16[16,32,384]{2,1,0:T(8,128)(2,1)} %add_shares.1), calls=%async_computation.5 | async-start | bytes 786432 | tf_op jit(solution)/shard_map/all_to_all | solution.py:449
  108.4 6.5 %feature_grads.1 = bf16[2048,512]{1,0:T(8,128)(2,1)} custom-call(s32[1,512]{1,0:T(1,128)} %pix_ref.5, f32[512,256]{1,0:T(8,128)} %copy-done.7, bf16[512,256]{1,0:T(8,128)(2,1)} %proj_ref.5, bf16[2048,124]{1,0:T(8,128)(2,1)} %copy-done.11, bf16[512,124]{1,0:T(8,128)(2,1)} %class_ref.1), custom_call_target="tpu_custom_call" | custom-call | flops 2407530496 | bytes 4194304 | tf_op jit(solution)/shard_map/feature_grads/pallas_call | solution.py:552
  114.9 2.6 %all-to-all-done.5 = bf16[16,32,384]{2,1,0:T(8,128)(2,1)S(1)} async-done(((bf16[16,32,384]{2,1,0:T(8,128)(2,1)}), bf16[16,32,384]{2,1,0:T(8,128)(2,1)S(1)}, u32[]{:S(2)}, u32[]{:S(2)}) %all-to-all-start.5) | async-done | bytes 393248 | tf_op jit(solution)/shard_map/all_to_all | solution.py:449
  117.5 1.5 %outputs.1 = (f32[512,256]{1,0:T(8,128)}, f32[512,124]{1,0:T(8,128)}, f32[2]{0:T(128)}) custom-call(s32[16]{0:T(128)S(1)} %copy-done.14, bf16[512,384]{1,0:T(8,128)(2,1)S(1)} %bitcast.9), custom_call_target="tpu_custom_call" | custom-call | bytes 1171528 | tf_op jit(solution)/shard_map/outputs/pallas_call | solution.py:436
  (11 shorter events, 0.0 us)
Async XLA Ops:
  0.6 12.1 %copy-start.14 = (s32[16]{0:T(128)S(1)}, s32[16]{0:T(128)}, u32[]{:S(2)}) copy-start(s32[16]{0:T(128)} %blocks_ref.14) | copy-start | bytes 196
  5.6 15.6 %all-to-all-start.1 = ((bf16[16,32,256]{2,1,0:T(8,128)(2,1)}), bf16[16,32,256]{2,1,0:T(8,128)(2,1)S(1)}, u32[]{:S(2)}, u32[]{:S(2)}) async-start(bf16[16,32,256]{2,1,0:T(8,128)(2,1)} %get-tuple-element.36), calls=%async_computation.1 | async-start | bytes 524288 | tf_op jit(solution)/shard_map/all_to_all | solution.py:449
  24.3 4.6 %copy-start.8 = (bf16[2048,512]{1,0:T(8,128)(2,1)S(1)}, bf16[2048,512]{1,0:T(8,128)(2,1)}, u32[]{:S(2)}) copy-start(bf16[2048,512]{1,0:T(8,128)(2,1)} %features_hbm.2) | copy-start | bytes 6291460
  24.3 4.6 %copy-start.12 = (bf16[512,124]{1,0:T(8,128)(2,1)S(1)}, bf16[512,124]{1,0:T(8,128)(2,1)}, u32[]{:S(2)}) copy-start(bf16[512,124]{1,0:T(8,128)(2,1)} %class_ref.1) | copy-start | bytes 380932
  24.3 39.5 %all-to-all-start.2 = ((bf16[16,320,256]{2,1,0:T(8,128)(2,1)}), bf16[16,320,256]{2,1,0:T(8,128)(2,1)}, u32[]{:S(2)}, u32[]{:S(2)}) async-start(bf16[16,320,256]{2,1,0:T(8,128)(2,1)} %pack_keys.3), calls=%async_computation.2 | async-start | bytes 5242880 | tf_op jit(solution)/shard_map/all_to_all | solution.py:449
  29.8 1.0 copy-start.10
  32.1 7.2 %copy-start.13 = (s32[2048]{0:T(1024)S(1)}, s32[2048]{0:T(1024)}, u32[]{:S(2)}) copy-start(s32[2048]{0:T(1024)} %param.15) | copy-start | bytes 24580
  37.8 5.8 %copy-start.9 = (bf16[2048,512]{1,0:T(8,128)(2,1)S(1)}, bf16[2048,512]{1,0:T(8,128)(2,1)}, u32[]{:S(2)}) copy-start(bf16[2048,512]{1,0:T(8,128)(2,1)} %features_hbm.2) | copy-start | bytes 6291460
  43.6 0.8 copy-start.11
  43.6 20.3 %copy-start = (bf16[512,256]{1,0:T(8,128)(2,1)S(1)}, bf16[512,256]{1,0:T(8,128)(2,1)}, u32[]{:S(2)}) copy-start(bf16[512,256]{1,0:T(8,128)(2,1)} %get-tuple-element.35.own_ref) | copy-start | bytes 786436
  43.6 20.3 %copy-start.6 = (f32[8,512]{1,0:T(8,128)S(1)}, f32[8,512]{1,0:T(8,128)}, u32[]{:S(2)}) copy-start(f32[8,512]{1,0:T(8,128)} %get-tuple-element.40.lanes_ref) | copy-start | bytes 49156
  63.8 10.6 %copy-start.1 = (f32[512,128]{1,0:T(8,128)S(1)}, f32[512,128]{1,0:T(8,128)}, u32[]{:S(2)}) copy-start(f32[512,128]{1,0:T(8,128)} %get-tuple-element.39.info_ref) | copy-start | bytes 786436
  63.9 10.6 %copy-start.2 = (f32[1,8192]{1,0:T(1,128)S(1)}, f32[1,8192]{1,0:T(1,128)}, u32[]{:S(2)}) copy-start(f32[1,8192]{1,0:T(1,128)} %get-tuple-element.42.key_label_ref) | copy-start | bytes 98308
  70.3 11.8 %all-to-all-start.3 = ((f32[16,4,128]{2,1,0:T(4,128)}), f32[16,4,128]{2,1,0:T(4,128)S(1)}, u32[]{:S(2)}, u32[]{:S(2)}) async-start(f32[16,4,128]{2,1,0:T(4,128)} %get-tuple-element.44), calls=%async_computation.3 | async-start | bytes 65536 | tf_op jit(solution)/shard_map/all_to_all | solution.py:449
  74.5 7.6 %copy-start.3 = (f32[512,256]{1,0:T(8,128)S(1)}, f32[512,256]{1,0:T(8,128)}, u32[]{:S(2)}) copy-start(f32[512,256]{1,0:T(8,128)} %get-tuple-element.47.unit_hbm) | copy-start | bytes 1572868
  74.5 7.6 %copy-start.4 = (bf16[512,512]{1,0:T(8,128)(2,1)S(1)}, bf16[512,512]{1,0:T(8,128)(2,1)}, u32[]{:S(2)}) copy-start(bf16[512,512]{1,0:T(8,128)(2,1)} %get-tuple-element.49.picked_hbm) | copy-start | bytes 1572868
  74.5 7.6 %copy-start.5 = (f32[512,128]{1,0:T(8,128)S(1)}, f32[512,128]{1,0:T(8,128)}, u32[]{:S(2)}) copy-start(f32[512,128]{1,0:T(8,128)} %get-tuple-element.48.length_hbm) | copy-start | bytes 786436
  88.8 15.9 %copy-start.7 = (f32[512,256]{1,0:T(8,128)}, f32[512,256]{1,0:T(8,128)S(1)}, u32[]{:S(2)}) copy-start(f32[512,256]{1,0:T(8,128)S(1)} %get-tuple-element.50.grad_ref) | copy-start | bytes 1572868
  104.7 12.8 %all-to-all-start.5 = ((bf16[16,32,384]{2,1,0:T(8,128)(2,1)}), bf16[16,32,384]{2,1,0:T(8,128)(2,1)S(1)}, u32[]{:S(2)}, u32[]{:S(2)}) async-start(bf16[16,32,384]{2,1,0:T(8,128)(2,1)} %add_shares.1), calls=%async_computation.5 | async-start | bytes 786432 | tf_op jit(solution)/shard_map/all_to_all | solution.py:449

commit v5 on v4

--- a/solution.py
+++ b/solution.py
@@ -8,12 +8,11 @@
 from jax.sharding import PartitionSpec as P
 
 BLK = 128
-SOON = (0, 4, 12)
+SOON = (0, 2, 8)
 UNIT = 16
 PARTS = BLK // UNIT
-TILE = 1024
+TILE = 512
 ROOM = 40
-PAIRS = TILE // (2 * BLK)
 INV_TEMP = 10.0
 EXP_SCALE = INV_TEMP * 1.4426950408889634
 NORM_EPS = 1e-06
@@ -213,7 +212,7 @@
         copies = copies_of(which, keys_hbm, start, end - start, start)
         for copy in copies:
             copy.start()
-        waits[start // PAIRS] = copies
+        waits[start // 2] = copies
     last = copies_of(len(SOON), more_hbm, 0, more, units)
 
     @pl.when(valid > ROOM)
@@ -244,7 +243,7 @@
 
 
 def key_tile_of(keys, tile):
-    return keys[pl.ds(PAIRS * tile, PAIRS)].reshape(TILE, keys.shape[-1])
+    return keys[pl.ds(2 * tile, 2)].reshape(TILE, keys.shape[-1])
 
 
 def lanes_of(tile):

time: 120 us -> 119 us (level)
  Pallas kernels: 39.9 us -> 38.5 us
    pallas_call x9, Pallas kernels: 33.4 us -> 32 us  [call(): pl.pallas_call(kernel, name=name, out_shape=outs, in_specs=[s for _, s in...]
where the time goes in v5:
time: 119 us; the launch traced here: 118 us
  Pallas kernels  38.5 us (32%)
  waiting for transfers between devices  32 us (27%)
  starting transfers between devices  19.5 us (16%)
  blocking collectives  15 us (13%)
  other arithmetic  6.38 us (5%)
  local copies, waits for them, and re-layouts  3.05 us (3%)
  between operations  1.74 us (1%)
  matrix products  1.59 us (1%)
    pallas_call x9, Pallas kernels, call(): pl.pallas_call(kernel, name=name, out_shape=outs, in_specs=[s for _, s in...  32 us
    all_to_all x4, waiting for transfers between devices, exchange(): return lax.all_to_all(value, 'group', 0, 0, tiled=True)  32 us
    all_to_all x4, starting transfers between devices, exchange(): return lax.all_to_all(value, 'group', 0, 0, tiled=True)  19.5 us
    all_to_all x1, blocking collectives, exchange(): return lax.all_to_all(value, 'group', 0, 0, tiled=True)  15 us
    pallas_call x1, Pallas kernels, per_device(): pl.pallas_call(features_kernel, name='feature_grads', grid=(pixels // til...  6.5 us
    reduce_sum x2, other arithmetic, per_device(): pixel_loss = jnp.sum(logsum_class[:, 0] - jnp.sum(onehot * logits, axis=1))  2.47 us
  transfers between devices with their start and end apart: 4, of which 4 were waited for; matrix products, arithmetic and copies ran while one was open for 8% of the time, Pallas kernels for 14%

profile of v5, /device:TPU:128, one launch (start us, length us, event | category | flops | bytes accessed | tf_op | source)
XLA Modules:
  0.0 117.8 jit_solution(16218058013431610658)
XLA Ops:
  0.6 0.0 copy-start.14
  0.6 5.0 %pick_anchors.1 = (bf16[512,256]{1,0:T(8,128)(2,1)}, bf16[16,32,256]{2,1,0:T(8,128)(2,1)}) custom-call(s32[16]{0:T(128)} %blocks_ref.14, s32[1,512]{1,0:T(1,128)} %pix_ref.5, bf16[2048,512]{1,0:T(8,128)(2,1)} %features_hbm.2, bf16[512,256]{1,0:T(8,128)(2,1)} %proj_ref.5), custom_call_target="tpu_custom_call" | custom-call | flops 1207959552 | bytes 2885696 | tf_op jit(solution)/shard_map/pick_anchors/pallas_call | solution.py:435
  5.6 7.1 %all-to-all-start.1 = ((bf16[16,32,256]{2,1,0:T(8,128)(2,1)}), bf16[16,32,256]{2,1,0:T(8,128)(2,1)S(1)}, u32[]{:S(2)}, u32[]{:S(2)}) async-start(bf16[16,32,256]{2,1,0:T(8,128)(2,1)} %get-tuple-element.36), calls=%async_computation.1 | async-start | bytes 524288 | tf_op jit(solution)/shard_map/all_to_all | solution.py:448
  12.7 0.0 copy-done.14
  12.7 0.6 reduce_sum.36
  14.0 7.2 %all-to-all-done.1.recv_ref = bf16[16,32,256]{2,1,0:T(8,128)(2,1)S(1)} async-done(((bf16[16,32,256]{2,1,0:T(8,128)(2,1)}), bf16[16,32,256]{2,1,0:T(8,128)(2,1)S(1)}, u32[]{:S(2)}, u32[]{:S(2)}) %all-to-all-start.1) | async-done | bytes 262176 | tf_op jit(solution)/shard_map/all_to_all | solution.py:448
  21.2 0.5 conditional.1
  21.2 0.5 skip_keys.1
  21.8 2.5 %pack_keys.3 = bf16[16,320,256]{2,1,0:T(8,128)(2,1)} custom-call(s32[16]{0:T(128)S(1)} %copy-done.14, bf16[16,32,256]{2,1,0:T(8,128)(2,1)S(1)} %all-to-all-done.1.recv_ref), custom_call_target="tpu_custom_call" | custom-call | bytes 2883648 | tf_op jit(solution)/shard_map/pack_keys/pallas_call | solution.py:435
  24.3 0.0 copy-start.8
  24.3 0.0 copy-start.12
  24.3 4.6 %all-to-all-start.2 = ((bf16[16,320,256]{2,1,0:T(8,128)(2,1)}), bf16[16,320,256]{2,1,0:T(8,128)(2,1)}, u32[]{:S(2)}, u32[]{:S(2)}) async-start(bf16[16,320,256]{2,1,0:T(8,128)(2,1)} %pack_keys.3), calls=%async_computation.2 | async-start | bytes 5242880 | tf_op jit(solution)/shard_map/all_to_all | solution.py:448
  28.9 0.0 copy-done.8
  29.0 0.0 copy-done.12
  29.0 0.8 fusion
  29.8 0.0 copy-start.10
  29.8 1.0 copy-done.10
  30.8 1.3 %copy.11 = f32[2048,124]{1,0:T(8,128)} copy(f32[2048,124]{0,1:T(8,128)S(1)} %get-tuple-element.58) | data formatting | bytes 2031616 | tf_op jit(solution)/shard_map/dot_general | solution.py:508
  32.1 5.6 %anchor_labels.1 = (f32[1,8192]{1,0:T(1,128)}, f32[512,128]{1,0:T(8,128)}, f32[8,512]{1,0:T(8,128)}, f32[512,256]{1,0:T(8,128)}, f32[512,128]{1,0:T(8,128)}, /*index=5*/bf16[512,512]{1,0:T(8,128)(2,1)}) custom-call(s32[16]{0:T(128)S(1)} %copy-done.14, s32[16,512]{1,0:T(8,128)} %labels_ref, s32[1,512]{1,0:T(1,128)} %pix_ref.5, ...), custom_call_target="tpu_custom_call" | custom-call | bytes 4016192 | tf_op jit(solution)/shard_map/anchor_labels/pallas_call | solution.py:435
  37.8 0.0 copy-start.9
  37.8 1.5 %exponential_reduce_fusion = f32[2048]{0:T(1024)S(1)} fusion(f32[2048,124]{0,1:T(8,128)} %copy-done.10, f32[2048]{0:T(1024)S(1)} %get-tuple-element.57), kind=kLoop, calls=%fused_computation.3 | loop fusion | flops 505856 | bytes 1032192 | tf_op jit(solution)/shard_map/reduce_sum | solution.py:510
  39.3 0.0 copy-done.13
  39.3 1.9 %select_reduce_fusion = f32[2048]{0:T(1024)S(1)} fusion(f32[2048,124]{1,0:T(8,128)} %copy.11, s32[2048]{0:T(1024)S(1)} %copy-done.13), kind=kLoop, calls=%fused_computation | loop fusion | flops 759808 | bytes 1032192 | tf_op jit(solution)/shard_map/reduce_sum | solution.py:513
  41.2 0.6 subtract_reduce_fusion
  41.8 1.8 %subtract_convert_fusion.logits_ref = bf16[2048,124]{1,0:T(8,128)(2,1)S(1)} fusion(f32[2048,124]{1,0:T(8,128)} %copy.11, s32[2048]{0:T(1024)S(1)} %copy-done.13, f32[2048]{0:T(1024)S(1)} %get-tuple-element.56), kind=kLoop, calls=%fused_computation.1 | loop fusion | flops 1269760 | bytes 1540096 | tf_op jit(solution)/shard_map/convert_element_type | solution.py:514
  43.6 0.0 copy-done.9
  43.6 0.0 copy-start.11
  43.6 0.0 copy-start
  43.6 0.0 copy-start.6
  43.6 0.7 fusion.1
  44.4 0.0 copy-done.11
  44.4 0.7 concatenate.3.class_hbm
  45.0 18.8 %all-to-all-done.2 = bf16[16,320,256]{2,1,0:T(8,128)(2,1)} async-done(((bf16[16,320,256]{2,1,0:T(8,128)(2,1)}), bf16[16,320,256]{2,1,0:T(8,128)(2,1)}, u32[]{:S(2)}, u32[]{:S(2)}) %all-to-all-start.2) | async-done | bytes 2621472 | tf_op jit(solution)/shard_map/all_to_all | solution.py:448
  63.8 0.0 copy-done
  63.8 5.8 %anchor_sums.1 = (f32[512,128]{1,0:T(8,128)S(1)}, f32[16,4,128]{2,1,0:T(4,128)}) custom-call(s32[16]{0:T(128)S(1)} %copy-done.14, f32[8,512]{1,0:T(8,128)S(1)} %copy-done.6, bf16[512,256]{1,0:T(8,128)(2,1)S(1)} %copy-done, bf16[16,20,16,256]{3,2,1,0:T(8,128)(2,1)} %bitcast.2.keys_hbm, bf16[16,12,16,256]{3,2,1,0:T(8,128)(2,1)} %get-tuple-element.59.more_hbm), custom_call_target="tpu_custom_call" | custom-call | flops 1342177280 | bytes 4767808 | tf_op jit(solution)/shard_map/anchor_sums/pallas_call | solution.py:435
  69.7 4.2 %all-to-all-start.3 = ((f32[16,4,128]{2,1,0:T(4,128)}), f32[16,4,128]{2,1,0:T(4,128)S(1)}, u32[]{:S(2)}, u32[]{:S(2)}) async-start(f32[16,4,128]{2,1,0:T(4,128)} %get-tuple-element.44), calls=%async_computation.3 | async-start | bytes 65536 | tf_op jit(solution)/shard_map/all_to_all | solution.py:448
  73.9 0.0 copy-start.3
  73.9 4.2 %anchor_rows.1 = (f32[512,256]{1,0:T(8,128)S(1)}, f32[512,128]{1,0:T(8,128)S(1)}, f32[8,128]{1,0:T(8,128)S(1)}) custom-call(s32[16]{0:T(128)S(1)} %copy-done.14, bf16[512,256]{1,0:T(8,128)(2,1)S(1)} %copy-done, f32[512,128]{1,0:T(8,128)S(1)} %copy-done.1, f32[512,128]{1,0:T(8,128)S(1)} %get-tuple-element.41.acc_ref, f32[1,8192]{1,0:T(1,128)S(1)} %copy-done.2, ...), custom_call_target="tpu_custom_call" | custom-call | flops 335544320 | bytes 5804096 | tf_op jit(solution)/shard_map/anchor_rows/pallas_call | solution.py:435
  78.1 3.4 %all-to-all-done.3.scales_ref = f32[16,4,128]{2,1,0:T(4,128)S(1)} async-done(((f32[16,4,128]{2,1,0:T(4,128)}), f32[16,4,128]{2,1,0:T(4,128)S(1)}, u32[]{:S(2)}, u32[]{:S(2)}) %all-to-all-start.3) | async-done | bytes 32800 | tf_op jit(solution)/shard_map/all_to_all | solution.py:448
  81.5 0.0 copy-done.3
  81.5 5.9 %anchor_keys.1 = (f32[512,256]{1,0:T(8,128)S(1)}, f32[512,384]{1,0:T(8,128)S(1)}) custom-call(s32[16]{0:T(128)S(1)} %copy-done.14, bf16[512,256]{1,0:T(8,128)(2,1)S(1)} %copy-done, f32[512,128]{1,0:T(8,128)S(1)} %get-tuple-element.43.row_scale_ref, f32[16,4,128]{2,1,0:T(4,128)S(1)} %all-to-all-done.3.scales_ref, f32[8,128]{1,0:T(8,128)S(1)} %get-tuple-element.45.loss_ref, ...), custom_call_target="tpu_custom_call" | custom-call | flops 2684354560 | bytes 8163392 | tf_op jit(solution)/shard_map/anchor_keys/pallas_call | solution.py:435
  87.4 0.0 copy-start.7
  87.4 15.0 %all_to_all.30.recv_ref = f32[16,32,384]{2,1,0:T(8,128)S(1)} all-to-all(f32[16,32,384]{2,1,0:T(8,128)S(1)} %bitcast.10), channel_id=1, replica_groups=mesh['dp'=16,'group'=16] {'group'}, dimensions={0} | all-to-all | bytes 1572864 | tf_op jit(solution)/shard_map/all_to_all | solution.py:448
  102.4 0.9 add_shares.1
  103.4 3.6 %all-to-all-start.5 = ((bf16[16,32,384]{2,1,0:T(8,128)(2,1)}), bf16[16,32,384]{2,1,0:T(8,128)(2,1)S(1)}, u32[]{:S(2)}, u32[]{:S(2)}) async-start(bf16[16,32,384]{2,1,0:T(8,128)(2,1)} %add_shares.1), calls=%async_computation.5 | async-start | bytes 786432 | tf_op jit(solution)/shard_map/all_to_all | solution.py:448
  107.0 6.5 %feature_grads.1 = bf16[2048,512]{1,0:T(8,128)(2,1)} custom-call(s32[1,512]{1,0:T(1,128)} %pix_ref.5, f32[512,256]{1,0:T(8,128)} %copy-done.7, bf16[512,256]{1,0:T(8,128)(2,1)} %proj_ref.5, bf16[2048,124]{1,0:T(8,128)(2,1)} %copy-done.11, bf16[512,124]{1,0:T(8,128)(2,1)} %class_ref.1), custom_call_target="tpu_custom_call" | custom-call | flops 2407530496 | bytes 4194304 | tf_op jit(solution)/shard_map/feature_grads/pallas_call | solution.py:551
  113.5 2.6 %all-to-all-done.5 = bf16[16,32,384]{2,1,0:T(8,128)(2,1)S(1)} async-done(((bf16[16,32,384]{2,1,0:T(8,128)(2,1)}), bf16[16,32,384]{2,1,0:T(8,128)(2,1)S(1)}, u32[]{:S(2)}, u32[]{:S(2)}) %all-to-all-start.5) | async-done | bytes 393248 | tf_op jit(solution)/shard_map/all_to_all | solution.py:448
  116.2 1.5 %outputs.1 = (f32[512,256]{1,0:T(8,128)}, f32[512,124]{1,0:T(8,128)}, f32[2]{0:T(128)}) custom-call(s32[16]{0:T(128)S(1)} %copy-done.14, bf16[512,384]{1,0:T(8,128)(2,1)S(1)} %bitcast.9), custom_call_target="tpu_custom_call" | custom-call | bytes 1171528 | tf_op jit(solution)/shard_map/outputs/pallas_call | solution.py:435
  (11 shorter events, 0.0 us)
Async XLA Ops:
  0.6 12.1 %copy-start.14 = (s32[16]{0:T(128)S(1)}, s32[16]{0:T(128)}, u32[]{:S(2)}) copy-start(s32[16]{0:T(128)} %blocks_ref.14) | copy-start | bytes 196
  5.6 15.6 %all-to-all-start.1 = ((bf16[16,32,256]{2,1,0:T(8,128)(2,1)}), bf16[16,32,256]{2,1,0:T(8,128)(2,1)S(1)}, u32[]{:S(2)}, u32[]{:S(2)}) async-start(bf16[16,32,256]{2,1,0:T(8,128)(2,1)} %get-tuple-element.36), calls=%async_computation.1 | async-start | bytes 524288 | tf_op jit(solution)/shard_map/all_to_all | solution.py:448
  24.3 4.6 %copy-start.8 = (bf16[2048,512]{1,0:T(8,128)(2,1)S(1)}, bf16[2048,512]{1,0:T(8,128)(2,1)}, u32[]{:S(2)}) copy-start(bf16[2048,512]{1,0:T(8,128)(2,1)} %features_hbm.2) | copy-start | bytes 6291460
  24.3 4.6 %copy-start.12 = (bf16[512,124]{1,0:T(8,128)(2,1)S(1)}, bf16[512,124]{1,0:T(8,128)(2,1)}, u32[]{:S(2)}) copy-start(bf16[512,124]{1,0:T(8,128)(2,1)} %class_ref.1) | copy-start | bytes 380932
  24.3 39.5 %all-to-all-start.2 = ((bf16[16,320,256]{2,1,0:T(8,128)(2,1)}), bf16[16,320,256]{2,1,0:T(8,128)(2,1)}, u32[]{:S(2)}, u32[]{:S(2)}) async-start(bf16[16,320,256]{2,1,0:T(8,128)(2,1)} %pack_keys.3), calls=%async_computation.2 | async-start | bytes 5242880 | tf_op jit(solution)/shard_map/all_to_all | solution.py:448
  29.8 1.0 copy-start.10
  32.1 7.2 %copy-start.13 = (s32[2048]{0:T(1024)S(1)}, s32[2048]{0:T(1024)}, u32[]{:S(2)}) copy-start(s32[2048]{0:T(1024)} %param.15) | copy-start | bytes 24580
  37.8 5.8 %copy-start.9 = (bf16[2048,512]{1,0:T(8,128)(2,1)S(1)}, bf16[2048,512]{1,0:T(8,128)(2,1)}, u32[]{:S(2)}) copy-start(bf16[2048,512]{1,0:T(8,128)(2,1)} %features_hbm.2) | copy-start | bytes 6291460
  43.6 0.8 copy-start.11
  43.6 20.2 %copy-start = (bf16[512,256]{1,0:T(8,128)(2,1)S(1)}, bf16[512,256]{1,0:T(8,128)(2,1)}, u32[]{:S(2)}) copy-start(bf16[512,256]{1,0:T(8,128)(2,1)} %get-tuple-element.35.own_ref) | copy-start | bytes 786436
  43.6 20.2 %copy-start.6 = (f32[8,512]{1,0:T(8,128)S(1)}, f32[8,512]{1,0:T(8,128)}, u32[]{:S(2)}) copy-start(f32[8,512]{1,0:T(8,128)} %get-tuple-element.40.lanes_ref) | copy-start | bytes 49156
  63.8 10.0 %copy-start.1 = (f32[512,128]{1,0:T(8,128)S(1)}, f32[512,128]{1,0:T(8,128)}, u32[]{:S(2)}) copy-start(f32[512,128]{1,0:T(8,128)} %get-tuple-element.39.info_ref) | copy-start | bytes 786436
  63.8 10.0 %copy-start.2 = (f32[1,8192]{1,0:T(1,128)S(1)}, f32[1,8192]{1,0:T(1,128)}, u32[]{:S(2)}) copy-start(f32[1,8192]{1,0:T(1,128)} %get-tuple-element.42.key_label_ref) | copy-start | bytes 98308
  69.7 11.8 %all-to-all-start.3 = ((f32[16,4,128]{2,1,0:T(4,128)}), f32[16,4,128]{2,1,0:T(4,128)S(1)}, u32[]{:S(2)}, u32[]{:S(2)}) async-start(f32[16,4,128]{2,1,0:T(4,128)} %get-tuple-element.44), calls=%async_computation.3 | async-start | bytes 65536 | tf_op jit(solution)/shard_map/all_to_all | solution.py:448
  73.9 7.6 %copy-start.3 = (f32[512,256]{1,0:T(8,128)S(1)}, f32[512,256]{1,0:T(8,128)}, u32[]{:S(2)}) copy-start(f32[512,256]{1,0:T(8,128)} %get-tuple-element.47.unit_hbm) | copy-start | bytes 1572868
  73.9 7.6 %copy-start.4 = (bf16[512,512]{1,0:T(8,128)(2,1)S(1)}, bf16[512,512]{1,0:T(8,128)(2,1)}, u32[]{:S(2)}) copy-start(bf16[512,512]{1,0:T(8,128)(2,1)} %get-tuple-element.49.picked_hbm) | copy-start | bytes 1572868
  73.9 7.6 %copy-start.5 = (f32[512,128]{1,0:T(8,128)S(1)}, f32[512,128]{1,0:T(8,128)}, u32[]{:S(2)}) copy-start(f32[512,128]{1,0:T(8,128)} %get-tuple-element.48.length_hbm) | copy-start | bytes 786436
  87.4 16.0 %copy-start.7 = (f32[512,256]{1,0:T(8,128)}, f32[512,256]{1,0:T(8,128)S(1)}, u32[]{:S(2)}) copy-start(f32[512,256]{1,0:T(8,128)S(1)} %get-tuple-element.50.grad_ref) | copy-start | bytes 1572868
  103.4 12.8 %all-to-all-start.5 = ((bf16[16,32,384]{2,1,0:T(8,128)(2,1)}), bf16[16,32,384]{2,1,0:T(8,128)(2,1)S(1)}, u32[]{:S(2)}, u32[]{:S(2)}) async-start(bf16[16,32,384]{2,1,0:T(8,128)(2,1)} %add_shares.1), calls=%async_computation.5 | async-start | bytes 786432 | tf_op jit(solution)/shard_map/all_to_all | solution.py:448
